TPU v7x, 32 devices: a whole 2x2x4 slice. The times are simulated.
32 devices in a mesh: row: 4 (over y, x), col: 8 (over z, core).
Axes of the slice: x: 2, y: 2, z: 4, core: 2. Of those that a mesh axis runs over, the one named last changes fastest.
Arguments:
- out_grad: bfloat16 [512, 6144], P('row', 'col'), may hold values from -6 to 6
- hidden: bfloat16 [512, 24576], P('row'), may hold values from -0.1796875 to 0.1796875
- weight: bfloat16 [24576, 6144], P('row', 'col'), may hold values from -0.078125 to 0.078125
- compress: bfloat16 [512, 128], replicated, may hold values from -0.25 to 0.25
- feedback: bfloat16 [8, 512, 24576], P('col', None, 'row'), may hold values from -1.5 to 1.5
Outputs:
- grad_input: bfloat16 [512, 24576], P('col', 'row')
- grad_weight: bfloat16 [24576, 6144], P('row', 'col')
- new_feedback: bfloat16 [8, 512, 24576], P('col', None, 'row')
All inputs are finite; a program needn't handle non-finite values.
Results may differ from a plain program's by a relative error of at most 0.0056.
Values may be sent and summed in bfloat16 or wider, within the bound.
No kernel may reach another device: no remote copies, remote signals or barrier semaphores. Data moves between devices by JAX's collectives and lax.ppermute only.
A program may use at most 256 MiB of HBM per device.

v0:
```python
import jax
import jax.numpy as jnp
from jax import lax
from jax.sharding import PartitionSpec as P


def on_device(out_grad, hidden, weight, compress, feedback):
    grads = lax.all_gather(out_grad, "row", axis=0, tiled=True)
    tokens = grads.shape[0]
    units = weight.shape[0]
    nblocks = units // compress.shape[0]
    partial_value = lax.dot_general(
        grads, weight, (((1,), (1,)), ((), ())), preferred_element_type=jnp.float32
    )
    acc = partial_value + feedback[0].astype(jnp.float32)
    blocks = acc.astype(jnp.bfloat16).reshape(tokens, nblocks, compress.shape[0])
    code = jnp.einsum("tnb,bs->tns", blocks, compress, preferred_element_type=jnp.float32)
    code_low = code.astype(jnp.bfloat16)
    recon = jnp.einsum("tns,bs->tnb", code_low, compress, preferred_element_type=jnp.float32)
    new_feedback = (acc - recon.reshape(tokens, units)).astype(jnp.bfloat16)[None]
    flat_code = code.reshape(tokens, nblocks * compress.shape[1])
    total = lax.psum_scatter(flat_code, "col", scatter_dimension=0, tiled=True)
    mine = total.shape[0]
    total_low = total.astype(jnp.bfloat16).reshape(mine, nblocks, compress.shape[1])
    grad_input = jnp.einsum("tns,bs->tnb", total_low, compress, preferred_element_type=jnp.float32)
    grad_input = grad_input.reshape(mine, units).astype(jnp.bfloat16)
    grad_weight = lax.psum_scatter(
        lax.dot_general(
            hidden, out_grad, (((0,), (0,)), ((), ())), preferred_element_type=jnp.float32
        ),
        "row",
        scatter_dimension=0,
        tiled=True,
    ).astype(jnp.bfloat16)
    return (grad_input, grad_weight, new_feedback)


def solution(mesh):
    return jax.shard_map(
        on_device,
        mesh=mesh,
        in_specs=(P("row", "col"), P("row", None), P("row", "col"), P(), P("col", None, "row")),
        out_specs=(P("col", "row"), P("row", "col"), P("col", None, "row")),
        check_vma=False,
    )
```

profile of v0, /device:TPU:0, one launch (start us, length us, event | category | flops | bytes accessed | tf_op | source)
XLA Modules:
  0.0 736.7 jit_solution(17863933897187599507)
XLA Ops:
  7.2 0.0 copy-start
  7.2 0.0 reduce-scatter.3.cloned.1.call-start
  7.2 13.8 %all_gather.3 = bf16[512,768]{1,0:T(8,128)(2,1)S(1)} all-gather(bf16[128,768]{1,0:T(8,128)(2,1)} %param.5), channel_id=1, replica_groups=mesh['row'=4,'col'=8] {'row'}, dimensions={0}, use_global_device_ids=true | all-gather | bytes 983040 | tf_op jit(solution)/shard_map/all_gather | solution.py:8
  21.0 13.9 %fusion.10 = (bf16[512,6144]{1,0:T(8,128)(2,1)}, f32[512,6144]{1,0:T(8,128)}) fusion(bf16[1,512,6144]{2,1,0:T(8,128)(2,1)} %param.9, bf16[512,768]{1,0:T(8,128)(2,1)S(1)} %all_gather.3, bf16[6144,768]{1,0:T(8,128)(2,1)} %param.7), kind=kOutput, calls=%fused_computation.14 | convolution fusion | flops 4841275392 | bytes 35389440 | tf_op jit(solution)/shard_map/dot_general | solution.py:12
  34.9 8.6 %copy.12 = bf16[512,6144]{0,1:T(8,128)(2,1)} copy(bf16[512,6144]{1,0:T(8,128)(2,1)} %get-tuple-element.3) | data formatting | bytes 12582912 | tf_op jit(solution)/shard_map/convert_element_type | solution.py:16
  43.5 0.0 copy-done
  43.5 4.0 fusion.8
  47.5 0.0 copy-start.1
  47.5 2.4 copy.15
  49.9 0.0 reduce-scatter.3.cloned.1.call-update
  49.9 0.0 reduce-scatter.5.cloned.1.call-start
  50.0 0.0 copy-done.1
  50.0 30.5 %fusion.11 = f32[24576,768]{1,0:T(8,128)} fusion(bf16[128,24576]{1,0:T(8,128)(2,1)} %param.6, bf16[128,768]{1,0:T(8,128)(2,1)S(1)} %copy-done.1), kind=kOutput, calls=%fused_computation.15 | convolution fusion | flops 4831838208 | bytes 81985536 | tf_op jit(solution)/shard_map/dot_general | solution.py:28
  80.5 0.0 reduce-scatter.5.cloned.1.call-update
  80.5 6.3 fusion.1
  86.8 12.6 %copy.19 = f32[512,6144]{1,0:T(8,128)} copy(f32[512,6144]{0,1:T(8,128)} %bitcast.32) | data formatting | bytes 25165824 | tf_op jit(solution)/shard_map/reshape | solution.py:20
  99.5 12.4 %fusion = bf16[1,512,6144]{2,1,0:T(8,128)(2,1)} fusion(f32[512,6144]{1,0:T(8,128)} %get-tuple-element.4, f32[512,6144]{1,0:T(8,128)} %copy.19), kind=kLoop, calls=%fused_computation.2 | loop fusion | flops 6291456 | bytes 31457280 | tf_op jit(solution)/shard_map/broadcast_in_dim | solution.py:20
  111.8 0.0 reduce-scatter.3.cloned.1.call-done
  111.9 1.4 fusion.3
  113.3 1.0 copy.25
  114.2 604.5 %reduce-scatter.5.cloned.1.call-done = f32[6144,768]{1,0:T(8,128)} async-done(((f32[24576,768]{1,0:T(8,128)}), f32[6144,768]{1,0:T(8,128)}) %reduce-scatter.5.cloned.1.call-update) | async-done | bytes 18874384 | tf_op jit(solution)/shard_map/reduce_scatter | solution.py:27
  718.7 11.1 %convert_element_type.33 = bf16[6144,768]{1,0:T(8,128)(2,1)} convert(f32[6144,768]{1,0:T(8,128)} %reduce-scatter.5.cloned.1.call-done) | non-fusion elementwise | flops 4718592 | bytes 28311552 | tf_op jit(solution)/shard_map/convert_element_type | solution.py:34
Async XLA Ops:
  7.2 36.4 %copy-start = (bf16[512,128]{1,0:T(8,128)(2,1)S(1)}, bf16[512,128]{1,0:T(8,128)(2,1)}, u32[]{:S(2)}) copy-start(bf16[512,128]{1,0:T(8,128)(2,1)} %param.8) | copy-start | bytes 393220
  7.2 104.7 %reduce-scatter.3.cloned.1.call-start = ((), (), s32[]{:S(2)}) async-start(), calls=%async_computation.2 | async-start | bytes 3538944 | tf_op jit(solution)/shard_map/reduce_scatter | solution.py:22
  47.5 2.5 copy-start.1
  49.9 668.8 %reduce-scatter.5.cloned.1.call-start = ((), (), s32[]{:S(2)}) async-start(), calls=%async_computation.3 | async-start | bytes 94371840 | tf_op jit(solution)/shard_map/reduce_scatter | solution.py:27
Sparse Core Ops, SparseCore 0:
  50.0 40.6 reduce-scatter.2
  93.8 624.8 reduce-scatter.4
where the time goes:
time: 737 us
  waiting for transfers between devices  605 us (82%)
  matrix products  56.1 us (8%)
  local copies, waits for them, and re-layouts  24.6 us (3%)
  other arithmetic  23.5 us (3%)
  between operations  14.1 us (2%)
  blocking collectives  13.8 us (2%)
    reduce_scatter x1, waiting for transfers between devices, on_device(): lax.psum_scatter(lax.dot_general(hidden, out_grad, (((0,), (0,)), ((), ()...  604 us
    dot_general x1, matrix products, on_device(): lax.dot_general(hidden, out_grad, (((0,), (0,)), ((), ())), preferred_ele...  30.5 us
  transfers between devices with their start and end apart: 2, of which 1 were waited for; matrix products, arithmetic and copies ran while one was open for 9% of the time, Pallas kernels for 0%

commit v1 on v0

v1 whole, which is shorter than its diff:
```python
import functools

import jax
import jax.numpy as jnp
from jax import lax
from jax.experimental import pallas as pl
from jax.experimental.pallas import tpu as pltpu
from jax.sharding import PartitionSpec as P

F32 = jnp.float32
BF16 = jnp.bfloat16
MIB = 1024 * 1024
GW_BLOCKS = 4
LONG = pl.CostEstimate(flops=1 << 36, bytes_accessed=1 << 28, transcendentals=0)
COST = pl.CostEstimate(flops=1, bytes_accessed=1, transcendentals=0)


def in_hbm(*arrays):
    return [pltpu.with_memory_space_constraint(x, pltpu.HBM) for x in arrays]


def xor_perm(n, k):
    return [(i, i ^ k) for i in range(n)]


def place(i, count):
    bits = count.bit_length() - 1
    return sum(((i >> b) & 1) << (bits - 1 - b) for b in range(bits))


def compress_kernel(nrow, ncol, idx_ref, *refs):
    pieces = refs[:nrow]
    weight_ref, feedback_ref, compress_ref = refs[nrow : nrow + 3]
    fresh_ref, *code_refs, ordered_ref, grads, acc_buf, code_buf, sems = refs[nrow + 3 :]
    row, core = idx_ref[0], idx_ref[1]
    step_tokens = pieces[0].shape[0]
    blk, sub = compress_ref.shape
    count = weight_ref.shape[0] // blk

    def rows_at(i):
        return pl.ds(pl.multiple_of(i * step_tokens, step_tokens), step_tokens)

    def slot(k):
        if k == 0:
            return 0
        if k == nrow - 1:
            return 1
        return k + 1 + core if k % 2 else k - core + 1

    passed = [
        pltpu.make_async_copy(pieces[k], ordered_ref.at[rows_at(slot(k)), :], sems.at[k])
        for k in range(nrow)
    ]

    @pl.when(pl.program_id(0) == 0)
    def _():
        for copy in passed:
            copy.start()
        for k in range(nrow):
            grads[rows_at(row ^ k), :] = pieces[k][...]

    def product(b):
        cols = slice(b * blk, (b + 1) * blk)
        partial = lax.dot_general(
            grads[...], weight_ref[cols, :], (((1,), (1,)), ((), ())), preferred_element_type=F32
        )
        acc_buf[b] = partial + feedback_ref[0, :, cols].astype(F32)

    def finish(b):
        acc = acc_buf[b]
        code = jnp.dot(acc.astype(BF16), compress_ref[...], preferred_element_type=F32)
        code_low = code.astype(BF16)
        code_buf[:, b * sub : (b + 1) * sub] = code_low
        recon = lax.dot_general(
            code_low, compress_ref[...], (((1,), (1,)), ((), ())), preferred_element_type=F32
        )
        fresh_ref[0, :, b * blk : (b + 1) * blk] = (acc - recon).astype(BF16)

    for b in range(count):
        product(b)
        if b:
            finish(b - 1)
    finish(count - 1)

    mine_tokens = grads.shape[0] // ncol
    width = count * sub
    cols = pl.ds(pl.multiple_of(pl.program_id(0) * width, width), width)
    for i in range(ncol // 2):
        which, to = divmod(place(i, ncol // 2), ncol // 4)
        z = idx_ref[2] ^ i
        for whose, refs_of in ((core, code_refs[:2]), (1 - core, code_refs[2:])):
            at = pl.multiple_of((2 * z + whose) * mine_tokens, mine_tokens)
            refs_of[which][to * mine_tokens : (to + 1) * mine_tokens, cols] = code_buf[
                pl.ds(at, mine_tokens), :
            ]

    @pl.when(pl.program_id(0) == pl.num_programs(0) - 1)
    def _():
        for copy in passed:
            copy.wait()


def compress_call(idx, pieces, weight, feedback, compress, ncol):
    nrow = len(pieces)
    units, width = weight.shape
    blk, sub = compress.shape
    tokens = feedback.shape[1]
    nblocks = units // blk
    quarter = tokens // 4
    per = 3 if nblocks % 3 == 0 else 1
    return pl.pallas_call(
        functools.partial(compress_kernel, nrow, ncol),
        grid_spec=pltpu.PrefetchScalarGridSpec(
            num_scalar_prefetch=1,
            grid=(nblocks // per,),
            in_specs=[pl.BlockSpec((tokens // nrow, width), lambda j, s: (0, 0))]
            + [pl.BlockSpec(memory_space=pltpu.VMEM)] * (nrow - 1)
            + [
                pl.BlockSpec((per * blk, width), lambda j, s: (j, 0)),
                pl.BlockSpec((1, tokens, per * blk), lambda j, s: (0, 0, j)),
                pl.BlockSpec((blk, sub), lambda j, s: (0, 0)),
            ],
            out_specs=[pl.BlockSpec((1, tokens, per * blk), lambda j, s: (0, 0, j))]
            + [pl.BlockSpec(memory_space=pltpu.VMEM)] * 4
            + [pl.BlockSpec(memory_space=pl.ANY)],
            scratch_shapes=[
                pltpu.VMEM((tokens, width), BF16),
                pltpu.VMEM((per, tokens, blk), F32),
                pltpu.VMEM((tokens, per * sub), BF16),
                pltpu.SemaphoreType.DMA((nrow,)),
            ],
        ),
        out_shape=[pltpu.HBM((1, tokens, units), BF16)]
        + [jax.ShapeDtypeStruct((quarter, nblocks * sub), BF16)] * 4
        + [pltpu.HBM((tokens, width), BF16)],
        compiler_params=pltpu.CompilerParams(vmem_limit_bytes=30 * MIB),
        cost_estimate=LONG,
        name="compress_codes",
    )(idx, *in_hbm(pieces[0]), *pieces[1:], *in_hbm(weight, feedback, compress))


def pack_kernel(parts, idx_ref, hidden_ref, *refs):
    outs, (buf, sems) = refs[:-2], refs[-2:]
    arriving, leaving = [], []
    at = 0
    for i, (out, first, low, length) in enumerate(parts):
        source = pl.ds(pl.multiple_of(first(idx_ref[0], idx_ref[1]) + low, 128), length)
        held = buf.at[:, at : at + length]
        arriving.append(pltpu.make_async_copy(hidden_ref.at[:, source], held, sems.at[0, i]))
        leaving.append(
            pltpu.make_async_copy(held, outs[out].at[:, low : low + length], sems.at[1, i])
        )
        at += length
    for copy in arriving:
        copy.start()
    for copy, then in zip(arriving, leaving):
        copy.wait()
        then.start()
    for copy in leaving:
        copy.wait()


def pack_call(idx, hidden, firsts, lengths):
    step = min(lengths)
    parts = [
        (i, first, low, step)
        for i, (first, length) in enumerate(zip(firsts, lengths))
        for low in range(0, length, step)
    ]
    step_tokens = hidden.shape[0]
    return pl.pallas_call(
        functools.partial(pack_kernel, parts),
        grid_spec=pltpu.PrefetchScalarGridSpec(
            num_scalar_prefetch=1,
            grid=(1,),
            in_specs=[pl.BlockSpec(memory_space=pl.ANY)],
            out_specs=[pl.BlockSpec(memory_space=pl.ANY)] * len(firsts),
            scratch_shapes=[
                pltpu.VMEM((step_tokens, sum(lengths)), BF16),
                pltpu.SemaphoreType.DMA((2, len(parts))),
            ],
        ),
        out_shape=[pltpu.HBM((step_tokens, n), BF16) for n in lengths],
        compiler_params=pltpu.CompilerParams(vmem_limit_bytes=10 * MIB),
        cost_estimate=COST,
        name="pack_hidden",
    )(idx, *in_hbm(hidden))


def gw_kernel(npieces, steps, idx_ref, own_ref, diag_ref, swapped_ref, *refs):
    pieces = refs[:npieces]
    grads_ref = refs[npieces]
    out_ref, lhs = refs[-2:]
    step_tokens, block = own_ref.shape
    j = pl.program_id(0)
    core = idx_ref[1]

    def put(slot, x):
        lhs[slot * step_tokens : (slot + 1) * step_tokens, :] = x

    def columns(i):
        return pl.ds(pl.multiple_of(i * block, block), block)

    put(0, own_ref[...])
    for i, piece in enumerate(pieces):
        put(2 + i, piece[:, columns(gw_block(j, core, steps))])

    @pl.when(j < steps)
    def _():
        put(1, diag_ref[:, columns(j)])

    @pl.when(j >= steps)
    def _():
        put(1, swapped_ref[:, columns(j - steps)])

    out_ref[...] = lax.dot_general(
        lhs[...], grads_ref[...], (((0,), (0,)), ((), ())), preferred_element_type=F32
    ).astype(BF16)


def gw_block(j, core, steps):
    return jnp.where(j < steps, core, 1 - core) * steps + lax.rem(j, steps)


def gw_call(idx, hidden, diag, swapped, pieces, grads, prev, low, units):
    tokens, width = grads.shape
    step_tokens, half = diag.shape
    block = units // GW_BLOCKS
    steps = half // block
    at_low = low // block

    def at(j, s):
        return at_low + gw_block(j, s[1], steps)

    in_specs = [pl.BlockSpec((step_tokens, block), lambda j, s: (0, s[0] * GW_BLOCKS + at(j, s)))]
    in_specs += [pl.BlockSpec(memory_space=pltpu.VMEM)] * (2 + len(pieces))
    in_specs += [pl.BlockSpec((tokens, width), lambda j, s: (0, 0))]
    args = [*in_hbm(hidden), diag, swapped, *pieces, *in_hbm(grads)]
    aliases = {}
    if prev is not None:
        in_specs += [pl.BlockSpec(memory_space=pl.ANY)]
        args += [prev]
        aliases = {len(args): 0}
    return pl.pallas_call(
        functools.partial(gw_kernel, len(pieces), steps),
        grid_spec=pltpu.PrefetchScalarGridSpec(
            num_scalar_prefetch=1,
            grid=(2 * steps,),
            in_specs=in_specs,
            out_specs=pl.BlockSpec((block, width), lambda j, s: (at(j, s), 0)),
            scratch_shapes=[pltpu.VMEM((tokens, block), BF16)],
        ),
        out_shape=pltpu.HBM((units, width), BF16),
        input_output_aliases=aliases,
        compiler_params=pltpu.CompilerParams(vmem_limit_bytes=28 * MIB),
        cost_estimate=COST,
        name="weight_gradient",
    )(idx, *args)


def gi_kernel(own_ref, *refs):
    recv = refs[:-2]
    compress_ref, out_ref = refs[-2:]
    total = own_ref[...]
    for piece in recv:
        total = total + piece[...].astype(F32)
    low = total.astype(BF16)
    blk, sub = compress_ref.shape
    for n in range(low.shape[1] // sub):
        out_ref[:, n * blk : (n + 1) * blk] = lax.dot_general(
            low[:, n * sub : (n + 1) * sub],
            compress_ref[...],
            (((1,), (1,)), ((), ())),
            preferred_element_type=F32,
        ).astype(BF16)


def gi_call(own, recv, compress, units):
    tokens, codes = own.shape
    blk, sub = compress.shape
    nblocks = codes // sub
    per = nblocks // 3 if nblocks % 3 == 0 else 1
    spec = pl.BlockSpec((tokens, per * sub), lambda j: (0, j))
    return pl.pallas_call(
        gi_kernel,
        grid=(nblocks // per,),
        in_specs=[spec] * (1 + len(recv)) + [pl.BlockSpec((blk, sub), lambda j: (0, 0))],
        out_specs=pl.BlockSpec((tokens, per * blk), lambda j: (0, j)),
        out_shape=pltpu.HBM((tokens, units), BF16),
        compiler_params=pltpu.CompilerParams(vmem_limit_bytes=10 * MIB),
        cost_estimate=LONG,
        name="grad_input",
    )(own, *recv, compress)


def on_device(nrow, ncol, out_grad, hidden, weight, compress, feedback):
    row = lax.axis_index("row")
    col = lax.axis_index("col")
    core = col % 2
    units = weight.shape[0]
    step_tokens = out_grad.shape[0]
    after = lax.optimization_barrier

    def over_row(x, k):
        return lax.ppermute(x, "row", xor_perm(nrow, k))

    def over_col(x, k):
        return lax.ppermute(x, "col", xor_perm(ncol, k))

    idx = jnp.stack([row, core, col // 2]).astype(jnp.int32)
    grads = [out_grad] + [over_row(out_grad, k) for k in range(1, nrow)]

    def joint_perm(k):
        return [
            (r * ncol + c, (r ^ (k + c % 2)) * ncol + c) for r in range(nrow) for c in range(ncol)
        ]

    pairs = range(1, nrow - 1, 2)
    lows, lengths = [0, units // 2], [units // 2] * 2
    firsts, sizes = [], []
    for low, length in zip(lows, lengths):
        firsts += [lambda r, e, k=k, low=low: (r ^ (k + e)) * units + low for k in pairs]
        firsts += [
            lambda r, e, low=low, half=length // 2: (r ^ (nrow - 1)) * units + low + e * half
        ]
        sizes += [length] * len(pairs) + [length // 2]
    packed = pack_call(idx, hidden, firsts, sizes)

    def fetch(parts):
        fetched = [lax.ppermute(x, ("row", "col"), joint_perm(k)) for k, x in zip(pairs, parts)]
        return fetched + [over_row(parts[-1], nrow - 1)]

    def swap(parts):
        swapped = [over_col(x, 1) for x in parts]
        return parts[-1], swapped[-1], [x for pair in zip(parts[:-1], swapped[:-1]) for x in pair]

    early = fetch(packed[: len(pairs) + 1])
    new_feedback, *codes, ordered = compress_call(idx, grads, weight, feedback, compress, ncol)
    late = fetch(packed[len(pairs) + 1 :])

    *others, kept, send = after((*early, *[over_col(x, 1) for x in codes[2:]]))
    early = swap(others)
    kept, send = [x.astype(F32) + y.astype(F32) for x, y in zip(codes[:2], (kept, send))]
    step = 1
    while True:
        received = over_col(send.astype(BF16), 2 * step)
        step *= 2
        if step == ncol // 2:
            break
        size = kept.shape[0] // 2
        send = kept[size:] + received[size:].astype(F32)
        kept = kept[:size] + received[:size].astype(F32)

    grad_weight = gw_call(idx, hidden, *early, ordered, None, lows[0], units)
    grad_weight, kept, *late = after((grad_weight, kept, *late))
    grad_input = gi_call(kept, [received], compress, units)
    diag, swapped, pieces = swap(late)
    grad_input, swapped, *pieces = after((grad_input, swapped, *pieces))
    grad_weight = gw_call(idx, hidden, diag, swapped, pieces, ordered, grad_weight, lows[1], units)
    return (grad_input, grad_weight, new_feedback)


def solution(mesh):
    return jax.shard_map(
        functools.partial(on_device, mesh.shape["row"], mesh.shape["col"]),
        mesh=mesh,
        in_specs=(P("row", "col"), P("row", None), P("row", "col"), P(), P("col", None, "row")),
        out_specs=(P("col", "row"), P("row", "col"), P("col", None, "row")),
        check_vma=False,
    )
```

time: 737 us -> 63.7 us (0.09)
  waiting for transfers between devices: 605 us -> 13 us
  matrix products: 56.1 us -> 0 us
  Pallas kernels: 0 us -> 32 us
  local copies, waits for them, and re-layouts: 24.6 us -> 0.01 us
  other arithmetic: 23.5 us -> 0.34 us
  starting transfers between devices: 0.08 us -> 17.4 us
  blocking collectives: 13.8 us -> 0 us
  between operations: 14.1 us -> 0.71 us
    reduce_scatter x2 -> x0, waiting for transfers between devices: 605 us -> none  [the longest x1 604 us: on_device(): lax.psum_scatter(lax.dot_general(hidden, out_grad, (((0,), (0,)), ((), ()...]
    dot_general x5 -> x0, matrix products: 56.1 us -> none  [the longest x1 30.5 us: on_device(): lax.dot_general(hidden, out_grad, (((0,), (0,)), ((), ())), preferred_ele...]
    pallas_call x0 -> x5, Pallas kernels: none -> 32 us  [the longest x1 14.2 us: compress_call(): pl.pallas_call(functools.partial(compress_kernel, nrow, ncol), grid_spec=...]
    ppermute x0 -> x15, starting transfers between devices: none -> 17.4 us  [the longest x5 10.4 us: over_row(): return lax.ppermute(x, 'row', xor_perm(nrow, k))]
    reshape x2 -> x0, local copies, waits for them, and re-layouts: 15 us -> none  [the longest x1 12.6 us: on_device(): recon.reshape(tokens, units)]
    all_gather x1 -> x0, blocking collectives: 13.8 us -> none  [on_device(): grads = lax.all_gather(out_grad, 'row', axis=0, tiled=True)]
    ppermute x0 -> x15, waiting for transfers between devices: none -> 13 us  [the longest x8 9.3 us: over_col(): return lax.ppermute(x, 'col', xor_perm(ncol, k))]
    broadcast_in_dim x1 -> x0, other arithmetic: 12.4 us -> none  [on_device(): (acc - recon.reshape(tokens, units)).astype(jnp.bfloat16)[None]]
  transfers between devices with their start and end apart: 2 -> 15, of which waited for: 1 -> 3; matrix products, arithmetic and copies ran while one was open for 9% -> 1% of each run, Pallas kernels for 0% -> 40%
where the time goes in v1:
time: 63.7 us; the launch traced here: 63.5 us
  Pallas kernels  32 us (50%)
  starting transfers between devices  17.4 us (27%)
  waiting for transfers between devices  13 us (20%)
  between operations  0.71 us (1%)
    pallas_call x1, Pallas kernels, compress_call(): pl.pallas_call(functools.partial(compress_kernel, nrow, ncol), grid_spec=...  14.2 us
    pallas_call x2, Pallas kernels, gw_call(): pl.pallas_call(functools.partial(gw_kernel, len(pieces), steps), grid_spe...  12.7 us
    ppermute x5, starting transfers between devices, over_row(): return lax.ppermute(x, 'row', xor_perm(nrow, k))  10.4 us
    ppermute x8, waiting for transfers between devices, over_col(): return lax.ppermute(x, 'col', xor_perm(ncol, k))  9.3 us
    ppermute x8, starting transfers between devices, over_col(): return lax.ppermute(x, 'col', xor_perm(ncol, k))  5.94 us
    ppermute x5, waiting for transfers between devices, over_row(): return lax.ppermute(x, 'row', xor_perm(nrow, k))  3.69 us
    pallas_call x1, Pallas kernels, pack_call(): pl.pallas_call(functools.partial(pack_kernel, parts), grid_spec=pltpu.Pre...  3.03 us
    pallas_call x1, Pallas kernels, gi_call(): pl.pallas_call(gi_kernel, grid=(nblocks // per,), in_specs=[spec] * (1 +...  2.05 us
  transfers between devices with their start and end apart: 15, of which 3 were waited for; matrix products, arithmetic and copies ran while one was open for 1% of the time, Pallas kernels for 40%

profile of v1, /device:TPU:0, one launch (start us, length us, event | category | flops | bytes accessed | tf_op | source)
XLA Modules:
  0.0 63.5 jit_solution(4990742479794404907)
XLA Ops:
  0.6 3.0 %collective-permute-start.3 = (bf16[128,768]{1,0:T(8,128)(2,1)}, bf16[128,768]{1,0:T(8,128)(2,1)S(1)}, u32[]{:S(2)}, u32[]{:S(2)}) collective-permute-start(bf16[128,768]{1,0:T(8,128)(2,1)} %refs_0_.1), channel_id=1, source_target_pairs={{0,16},{8,24},{16,0},{24,8},{1,17},{9,25},{17,1},{25,9},{2,18},{10... | collective-permute-start | bytes 589832 | tf_op jit(solution)/shard_map/ppermute | solution.py:305
  3.7 1.5 %collective-permute-start.2 = (bf16[128,768]{1,0:T(8,128)(2,1)}, bf16[128,768]{1,0:T(8,128)(2,1)S(1)}, u32[]{:S(2)}, u32[]{:S(2)}) collective-permute-start(bf16[128,768]{1,0:T(8,128)(2,1)} %refs_0_.1), channel_id=1, source_target_pairs={{0,8},{8,0},{16,24},{24,16},{1,9},{9,1},{17,25},{25,17},{2,10},{10... | collective-permute-start | bytes 589832 | tf_op jit(solution)/shard_map/ppermute | solution.py:305
  5.2 0.1 collective-permute-start.4
  5.2 0.1 pad_add_fusion.idx_ref
  5.3 3.0 %pack_hidden.1 = (bf16[128,3072]{1,0:T(8,128)(2,1)}, bf16[128,1536]{1,0:T(8,128)(2,1)}, bf16[128,3072]{1,0:T(8,128)(2,1)}, bf16[128,1536]{1,0:T(8,128)(2,1)}) custom-call(s32[3]{0:T(128)S(1)} %pad_add_fusion.idx_ref, bf16[128,24576]{1,0:T(8,128)(2,1)} %own_ref.3), custom_call_target="tpu_custom_call" | custom-call | flops 1 | bytes 1 | tf_op jit(solution)/shard_map/pack_hidden/pallas_call | solution.py:171
  8.3 2.9 %collective-permute-start.1 = (bf16[128,1536]{1,0:T(8,128)(2,1)}, bf16[128,1536]{1,0:T(8,128)(2,1)S(1)}, u32[]{:S(2)}, u32[]{:S(2)}) collective-permute-start(bf16[128,1536]{1,0:T(8,128)(2,1)} %get-tuple-element.26), channel_id=1, source_target_pairs={{0,24},{8,16},{16,8},{24,0},{1,25},{9,17},{17,9},{25,1},{2,26},{10... | collective-permute-start | bytes 1179656 | tf_op jit(solution)/shard_map/ppermute | solution.py:305
  11.3 0.5 collective-permute-start
  11.8 0.0 collective-permute-done.3.refs_2_
  11.8 0.0 collective-permute-done.2.refs_1_
  11.8 3.7 %collective-permute-done.4.refs_3_ = bf16[128,768]{1,0:T(8,128)(2,1)S(1)} collective-permute-done((bf16[128,768]{1,0:T(8,128)(2,1)}, bf16[128,768]{1,0:T(8,128)(2,1)S(1)}, u32[]{:S(2)}, u32[]{:S(2)}) %collective-permute-start.4) | collective-permute-done | bytes 196640 | tf_op jit(solution)/shard_map/ppermute | solution.py:305
  15.5 14.2 %compress_codes.1 = (bf16[1,512,6144]{2,1,0:T(8,128)(2,1)}, bf16[128,1536]{1,0:T(8,128)(2,1)S(1)}, bf16[128,1536]{1,0:T(8,128)(2,1)S(1)}, bf16[128,1536]{1,0:T(8...) custom-call(s32[3]{0:T(128)S(1)} %pad_add_fusion.idx_ref, bf16[128,768]{1,0:T(8,128)(2,1)} %refs_0_.1, ...), custom_call_target="tpu_custom_call" | custom-call | flops 68719476736 | bytes 268435456 | tf_op jit(solution)/shard_map/compress_codes/pallas_call | solution.py:111
  29.7 0.1 collective-permute-start.5
  29.8 0.5 collective-permute-start.6
  30.3 2.9 %collective-permute-start.11 = (bf16[128,1536]{1,0:T(8,128)(2,1)S(1)}, bf16[128,1536]{1,0:T(8,128)(2,1)S(1)}, u32[]{:S(2)}, u32[]{:S(2)}) collective-permute-start(bf16[128,1536]{1,0:T(8,128)(2,1)S(1)} %copy-done.2), channel_id=1, source_target_pairs={{0,24},{8,16},{16,8},{24,0},{1,25},{9,17},{17,9},{25,1},{2,26},{10... | collective-permute-start | bytes 1179656 | tf_op jit(solution)/shard_map/ppermute | solution.py:305
  33.2 0.5 collective-permute-start.10
  33.8 0.1 add_convert_fusion
  33.9 1.6 %collective-permute-start.9 = (bf16[128,1536]{1,0:T(8,128)(2,1)S(1)}, bf16[128,1536]{1,0:T(8,128)(2,1)S(1)}, u32[]{:S(2)}, u32[]{:S(2)}) collective-permute-start(bf16[128,1536]{1,0:T(8,128)(2,1)S(1)} %add_convert_fusion), channel_id=1, source_target_pairs={{0,2},{1,3},{2,0},{3,1},{4,6},{5,7},{6,4},{7,5},{8,10},{9,11},{10,... | collective-permute-start | bytes 1179656 | tf_op jit(solution)/shard_map/ppermute | solution.py:308
  35.5 0.5 collective-permute-start.8
  36.0 0.1 convert_add_fusion
  36.1 8.3 %collective-permute-done.9 = bf16[128,1536]{1,0:T(8,128)(2,1)S(1)} collective-permute-done((bf16[128,1536]{1,0:T(8,128)(2,1)S(1)}, bf16[128,1536]{1,0:T(8,128)(2,1)S(1)}, u32[]{:S(2)}, u32[]{:S(2)}) %collective-permute-start.9) | collective-permute-done | bytes 393248 | tf_op jit(solution)/shard_map/ppermute | solution.py:308
  44.4 0.1 fusion
  44.5 2.6 %collective-permute-start.12 = (bf16[64,1536]{1,0:T(8,128)(2,1)S(1)}, bf16[64,1536]{1,0:T(8,128)(2,1)S(1)}, u32[]{:S(2)}, u32[]{:S(2)}) collective-permute-start(bf16[64,1536]{1,0:T(8,128)(2,1)S(1)} %get-tuple-element.47), channel_id=1, source_target_pairs={{0,4},{1,5},{2,6},{3,7},{4,0},{5,1},{6,2},{7,3},{8,12},{9,13},{10,... | collective-permute-start | bytes 589832 | tf_op jit(solution)/shard_map/ppermute | solution.py:308
  47.2 6.4 %weight_gradient.2.refs_3_ = bf16[6144,768]{1,0:T(8,128)(2,1)} custom-call(s32[3]{0:T(128)S(1)} %pad_add_fusion.idx_ref, bf16[128,24576]{1,0:T(8,128)(2,1)} %own_ref.3, bf16[128,1536]{1,0:T(8,128)(2,1)S(1)} %collective-permute-done.1.diag_ref, bf16[128,1536]{1,0:T(8,128)(2,1)S(1)} %collective-permute-done.7.swapped_ref, ...), custom_call_target="tpu_custom_call" | custom-call | flops 1 | bytes 1 | tf_op jit(solution)/shard_map/weight_gradient/pallas_call | solution.py:244
  53.5 0.0 collective-permute-done.11.diag_ref
  53.6 0.0 collective-permute-done.10.refs_0_
  53.6 0.1 collective-permute-start.13
  53.6 0.5 collective-permute-start.14
  54.1 1.0 %collective-permute-done.12.refs_0_ = bf16[64,1536]{1,0:T(8,128)(2,1)S(1)} collective-permute-done((bf16[64,1536]{1,0:T(8,128)(2,1)S(1)}, bf16[64,1536]{1,0:T(8,128)(2,1)S(1)}, u32[]{:S(2)}, u32[]{:S(2)}) %collective-permute-start.12) | collective-permute-done | bytes 196640 | tf_op jit(solution)/shard_map/ppermute | solution.py:308
  55.1 2.0 %grad_input.1 = bf16[64,6144]{1,0:T(8,128)(2,1)} custom-call(f32[64,1536]{1,0:T(8,128)S(1)} %get-tuple-element.38.own_ref, bf16[64,1536]{1,0:T(8,128)(2,1)S(1)} %collective-permute-done.12.refs_0_, bf16[512,128]{1,0:T(8,128)(2,1)S(1)} %copy-done), custom_call_target="tpu_custom_call" | custom-call | flops 68719476736 | bytes 268435456 | tf_op jit(solution)/shard_map/grad_input/pallas_call | solution.py:284
  57.1 0.0 collective-permute-done.13.swapped_ref
  57.1 0.0 collective-permute-done.14.refs_1_
  57.1 6.4 %weight_gradient.3 = bf16[6144,768]{1,0:T(8,128)(2,1)} custom-call(s32[3]{0:T(128)S(1)} %pad_add_fusion.idx_ref, bf16[128,24576]{1,0:T(8,128)(2,1)} %own_ref.3, bf16[128,1536]{1,0:T(8,128)(2,1)S(1)} %collective-permute-done.11.diag_ref, bf16[128,1536]{1,0:T(8,128)(2,1)S(1)} %collective-permute-done.13.swapped_ref, ...), custom_call_target="tpu_custom_call", output_to_operand_aliasing={{}: (7, {})} | custom-call | flops 1 | bytes 1 | tf_op jit(solution)/shard_map/weight_gradient/pallas_call | solution.py:244
  (13 shorter events, 0.0 us)
Async XLA Ops:
  0.6 11.2 %collective-permute-start.3 = (bf16[128,768]{1,0:T(8,128)(2,1)}, bf16[128,768]{1,0:T(8,128)(2,1)S(1)}, u32[]{:S(2)}, u32[]{:S(2)}) collective-permute-start(bf16[128,768]{1,0:T(8,128)(2,1)} %refs_0_.1), channel_id=1, source_target_pairs={{0,16},{8,24},{16,0},{24,8},{1,17},{9,25},{17,1},{25,9},{2,18},{10... | collective-permute-start | bytes 589832 | tf_op jit(solution)/shard_map/ppermute | solution.py:305
  3.7 8.1 %collective-permute-start.2 = (bf16[128,768]{1,0:T(8,128)(2,1)}, bf16[128,768]{1,0:T(8,128)(2,1)S(1)}, u32[]{:S(2)}, u32[]{:S(2)}) collective-permute-start(bf16[128,768]{1,0:T(8,128)(2,1)} %refs_0_.1), channel_id=1, source_target_pairs={{0,8},{8,0},{16,24},{24,16},{1,9},{9,1},{17,25},{25,17},{2,10},{10... | collective-permute-start | bytes 589832 | tf_op jit(solution)/shard_map/ppermute | solution.py:305
  5.2 10.3 %collective-permute-start.4 = (bf16[128,768]{1,0:T(8,128)(2,1)}, bf16[128,768]{1,0:T(8,128)(2,1)S(1)}, u32[]{:S(2)}, u32[]{:S(2)}) collective-permute-start(bf16[128,768]{1,0:T(8,128)(2,1)} %refs_0_.1), channel_id=1, source_target_pairs={{0,24},{8,16},{16,8},{24,0},{1,25},{9,17},{17,9},{25,1},{2,26},{10... | collective-permute-start | bytes 589832 | tf_op jit(solution)/shard_map/ppermute | solution.py:305
  8.3 24.9 %collective-permute-start.1 = (bf16[128,1536]{1,0:T(8,128)(2,1)}, bf16[128,1536]{1,0:T(8,128)(2,1)S(1)}, u32[]{:S(2)}, u32[]{:S(2)}) collective-permute-start(bf16[128,1536]{1,0:T(8,128)(2,1)} %get-tuple-element.26), channel_id=1, source_target_pairs={{0,24},{8,16},{16,8},{24,0},{1,25},{9,17},{17,9},{25,1},{2,26},{10... | collective-permute-start | bytes 1179656 | tf_op jit(solution)/shard_map/ppermute | solution.py:305
  11.3 19.0 %copy-start.2 = (bf16[128,1536]{1,0:T(8,128)(2,1)S(1)}, bf16[128,1536]{1,0:T(8,128)(2,1)}, u32[]{:S(2)}) copy-start(bf16[128,1536]{1,0:T(8,128)(2,1)} %get-tuple-element.37) | copy-start | bytes 1179652
  11.3 22.0 %copy-start.1 = (bf16[128,3072]{1,0:T(8,128)(2,1)S(1)}, bf16[128,3072]{1,0:T(8,128)(2,1)}, u32[]{:S(2)}) copy-start(bf16[128,3072]{1,0:T(8,128)(2,1)} %get-tuple-element.36) | copy-start | bytes 2359300
  11.3 22.5 %collective-permute-start = (bf16[128,3072]{1,0:T(8,128)(2,1)}, bf16[128,3072]{1,0:T(8,128)(2,1)S(1)}, u32[]{:S(2)}, u32[]{:S(2)}) collective-permute-start(bf16[128,3072]{1,0:T(8,128)(2,1)} %get-tuple-element.25), channel_id=1, source_target_pairs={{0,8},{1,17},{2,10},{3,19},{4,12},{5,21},{6,14},{7,23},{8,0},{9,25... | collective-permute-start | bytes 2359304 | tf_op jit(solution)/shard_map/ppermute | solution.py:330
  29.7 4.0 %collective-permute-start.5 = (bf16[128,1536]{1,0:T(8,128)(2,1)S(1)}, bf16[128,1536]{1,0:T(8,128)(2,1)S(1)}, u32[]{:S(2)}, u32[]{:S(2)}) collective-permute-start(bf16[128,1536]{1,0:T(8,128)(2,1)S(1)} %get-tuple-element.27), channel_id=1, source_target_pairs={{0,1},{1,0},{2,3},{3,2},{4,5},{5,4},{6,7},{7,6},{8,9},{9,8},{10,11... | collective-permute-start | bytes 1179656 | tf_op jit(solution)/shard_map/ppermute | solution.py:308
  29.8 4.0 %collective-permute-start.6 = (bf16[128,1536]{1,0:T(8,128)(2,1)S(1)}, bf16[128,1536]{1,0:T(8,128)(2,1)S(1)}, u32[]{:S(2)}, u32[]{:S(2)}) collective-permute-start(bf16[128,1536]{1,0:T(8,128)(2,1)S(1)} %get-tuple-element.28), channel_id=1, source_target_pairs={{0,1},{1,0},{2,3},{3,2},{4,5},{5,4},{6,7},{7,6},{8,9},{9,8},{10,11... | collective-permute-start | bytes 1179656 | tf_op jit(solution)/shard_map/ppermute | solution.py:308
  30.3 23.3 %collective-permute-start.11 = (bf16[128,1536]{1,0:T(8,128)(2,1)S(1)}, bf16[128,1536]{1,0:T(8,128)(2,1)S(1)}, u32[]{:S(2)}, u32[]{:S(2)}) collective-permute-start(bf16[128,1536]{1,0:T(8,128)(2,1)S(1)} %copy-done.2), channel_id=1, source_target_pairs={{0,24},{8,16},{16,8},{24,0},{1,25},{9,17},{17,9},{25,1},{2,26},{10... | collective-permute-start | bytes 1179656 | tf_op jit(solution)/shard_map/ppermute | solution.py:305
  33.2 20.3 %collective-permute-start.10 = (bf16[128,3072]{1,0:T(8,128)(2,1)S(1)}, bf16[128,3072]{1,0:T(8,128)(2,1)S(1)}, u32[]{:S(2)}, u32[]{:S(2)}) collective-permute-start(bf16[128,3072]{1,0:T(8,128)(2,1)S(1)} %copy-done.1), channel_id=1, source_target_pairs={{0,8},{1,17},{2,10},{3,19},{4,12},{5,21},{6,14},{7,23},{8,0},{9,25... | collective-permute-start | bytes 2359304 | tf_op jit(solution)/shard_map/ppermute | solution.py:330
  33.9 10.6 %collective-permute-start.9 = (bf16[128,1536]{1,0:T(8,128)(2,1)S(1)}, bf16[128,1536]{1,0:T(8,128)(2,1)S(1)}, u32[]{:S(2)}, u32[]{:S(2)}) collective-permute-start(bf16[128,1536]{1,0:T(8,128)(2,1)S(1)} %add_convert_fusion), channel_id=1, source_target_pairs={{0,2},{1,3},{2,0},{3,1},{4,6},{5,7},{6,4},{7,5},{8,10},{9,11},{10,... | collective-permute-start | bytes 1179656 | tf_op jit(solution)/shard_map/ppermute | solution.py:308
  35.5 11.7 %collective-permute-start.7 = (bf16[128,1536]{1,0:T(8,128)(2,1)S(1)}, bf16[128,1536]{1,0:T(8,128)(2,1)S(1)}, u32[]{:S(2)}, u32[]{:S(2)}) collective-permute-start(bf16[128,1536]{1,0:T(8,128)(2,1)S(1)} %collective-permute-done.1.diag_ref), channel_id=1, source_target_pairs={{0,1},{1,0},{2,3},{3,2},{4,5},{5,4},{6,7},{7,6},{8,9},{9,8},{10,11... | collective-permute-start | bytes 1179656 | tf_op jit(solution)/shard_map/ppermute | solution.py:308
  35.5 11.7 %collective-permute-start.8 = (bf16[128,3072]{1,0:T(8,128)(2,1)S(1)}, bf16[128,3072]{1,0:T(8,128)(2,1)S(1)}, u32[]{:S(2)}, u32[]{:S(2)}) collective-permute-start(bf16[128,3072]{1,0:T(8,128)(2,1)S(1)} %collective-permute-done.refs_0_), channel_id=1, source_target_pairs={{0,1},{1,0},{2,3},{3,2},{4,5},{5,4},{6,7},{7,6},{8,9},{9,8},{10,11... | collective-permute-start | bytes 2359304 | tf_op jit(solution)/shard_map/ppermute | solution.py:308
  44.5 10.6 %collective-permute-start.12 = (bf16[64,1536]{1,0:T(8,128)(2,1)S(1)}, bf16[64,1536]{1,0:T(8,128)(2,1)S(1)}, u32[]{:S(2)}, u32[]{:S(2)}) collective-permute-start(bf16[64,1536]{1,0:T(8,128)(2,1)S(1)} %get-tuple-element.47), channel_id=1, source_target_pairs={{0,4},{1,5},{2,6},{3,7},{4,0},{5,1},{6,2},{7,3},{8,12},{9,13},{10,... | collective-permute-start | bytes 589832 | tf_op jit(solution)/shard_map/ppermute | solution.py:308
  47.2 7.9 %copy-start = (bf16[512,128]{1,0:T(8,128)(2,1)S(1)}, bf16[512,128]{1,0:T(8,128)(2,1)}, u32[]{:S(2)}) copy-start(bf16[512,128]{1,0:T(8,128)(2,1)} %refs_1_.1) | copy-start | bytes 393220
  53.6 3.6 %collective-permute-start.13 = (bf16[128,1536]{1,0:T(8,128)(2,1)S(1)}, bf16[128,1536]{1,0:T(8,128)(2,1)S(1)}, u32[]{:S(2)}, u32[]{:S(2)}) collective-permute-start(bf16[128,1536]{1,0:T(8,128)(2,1)S(1)} %collective-permute-done.11.diag_ref), channel_id=1, source_target_pairs={{0,1},{1,0},{2,3},{3,2},{4,5},{5,4},{6,7},{7,6},{8,9},{9,8},{10,11... | collective-permute-start | bytes 1179656 | tf_op jit(solution)/shard_map/ppermute | solution.py:308
  53.6 3.5 %collective-permute-start.14 = (bf16[128,3072]{1,0:T(8,128)(2,1)S(1)}, bf16[128,3072]{1,0:T(8,128)(2,1)S(1)}, u32[]{:S(2)}, u32[]{:S(2)}) collective-permute-start(bf16[128,3072]{1,0:T(8,128)(2,1)S(1)} %collective-permute-done.10.refs_0_), channel_id=1, source_target_pairs={{0,1},{1,0},{2,3},{3,2},{4,5},{5,4},{6,7},{7,6},{8,9},{9,8},{10,11... | collective-permute-start | bytes 2359304 | tf_op jit(solution)/shard_map/ppermute | solution.py:308

commit v2 on v1

--- a/solution.py
+++ b/solution.py
@@ -10,7 +10,7 @@
 F32 = jnp.float32
 BF16 = jnp.bfloat16
 MIB = 1024 * 1024
-GW_BLOCKS = 4
+GW_BLOCKS = 8
 LONG = pl.CostEstimate(flops=1 << 36, bytes_accessed=1 << 28, transcendentals=0)
 COST = pl.CostEstimate(flops=1, bytes_accessed=1, transcendentals=0)
 
@@ -28,14 +28,16 @@
     return sum(((i >> b) & 1) << (bits - 1 - b) for b in range(bits))
 
 
-def compress_kernel(nrow, ncol, idx_ref, *refs):
-    pieces = refs[:nrow]
-    weight_ref, feedback_ref, compress_ref = refs[nrow : nrow + 3]
-    fresh_ref, *code_refs, ordered_ref, grads, acc_buf, code_buf, sems = refs[nrow + 3 :]
+def compress_kernel(nrow, ncol, group, idx_ref, *refs):
+    pieces = [refs[0], *refs[1:nrow]]
+    weight_hbm, feedback_hbm, compress_ref, fresh_hbm = refs[nrow : nrow + 4]
+    *code_refs, ordered_ref = refs[nrow + 4 : nrow + 9]
+    weight, feedback, fresh, grads, acc_buf, code_buf, in_sems, out_sems, sems = refs[nrow + 9 :]
     row, core = idx_ref[0], idx_ref[1]
     step_tokens = pieces[0].shape[0]
     blk, sub = compress_ref.shape
-    count = weight_ref.shape[0] // blk
+    nblocks = weight.shape[0]
+    mine_tokens = grads.shape[0] // ncol
 
     def rows_at(i):
         return pl.ds(pl.multiple_of(i * step_tokens, step_tokens), step_tokens)
@@ -47,26 +49,41 @@
             return 1
         return k + 1 + core if k % 2 else k - core + 1
 
+    def span(n):
+        return pl.ds(pl.multiple_of(n * blk, blk), blk)
+
+    def arriving(n):
+        return (
+            pltpu.make_async_copy(weight_hbm.at[span(n), :], weight.at[n], in_sems.at[0, n]),
+            pltpu.make_async_copy(feedback_hbm.at[0, :, span(n)], feedback.at[n], in_sems.at[1, n]),
+        )
+
+    def leaving(n):
+        return pltpu.make_async_copy(fresh.at[n], fresh_hbm.at[0, :, span(n)], out_sems.at[n])
+
+    @pl.loop(0, nblocks)
+    def _(n):
+        for copy in arriving(n):
+            copy.start()
+
     passed = [
         pltpu.make_async_copy(pieces[k], ordered_ref.at[rows_at(slot(k)), :], sems.at[k])
         for k in range(nrow)
     ]
-
-    @pl.when(pl.program_id(0) == 0)
-    def _():
-        for copy in passed:
-            copy.start()
-        for k in range(nrow):
-            grads[rows_at(row ^ k), :] = pieces[k][...]
-
-    def product(b):
-        cols = slice(b * blk, (b + 1) * blk)
+    for copy in passed:
+        copy.start()
+    for k in range(nrow):
+        grads[rows_at(row ^ k), :] = pieces[k][...]
+
+    def product(n, b):
+        for copy in arriving(n):
+            copy.wait()
         partial = lax.dot_general(
-            grads[...], weight_ref[cols, :], (((1,), (1,)), ((), ())), preferred_element_type=F32
+            grads[...], weight[n], (((1,), (1,)), ((), ())), preferred_element_type=F32
         )
-        acc_buf[b] = partial + feedback_ref[0, :, cols].astype(F32)
-
-    def finish(b):
+        acc_buf[b] = partial + feedback[n].astype(F32)
+
+    def finish(n, b):
         acc = acc_buf[b]
         code = jnp.dot(acc.astype(BF16), compress_ref[...], preferred_element_type=F32)
         code_low = code.astype(BF16)
@@ -74,30 +91,33 @@
         recon = lax.dot_general(
             code_low, compress_ref[...], (((1,), (1,)), ((), ())), preferred_element_type=F32
         )
-        fresh_ref[0, :, b * blk : (b + 1) * blk] = (acc - recon).astype(BF16)
-
-    for b in range(count):
-        product(b)
-        if b:
-            finish(b - 1)
-    finish(count - 1)
-
-    mine_tokens = grads.shape[0] // ncol
-    width = count * sub
-    cols = pl.ds(pl.multiple_of(pl.program_id(0) * width, width), width)
-    for i in range(ncol // 2):
-        which, to = divmod(place(i, ncol // 2), ncol // 4)
-        z = idx_ref[2] ^ i
-        for whose, refs_of in ((core, code_refs[:2]), (1 - core, code_refs[2:])):
-            at = pl.multiple_of((2 * z + whose) * mine_tokens, mine_tokens)
-            refs_of[which][to * mine_tokens : (to + 1) * mine_tokens, cols] = code_buf[
-                pl.ds(at, mine_tokens), :
-            ]
-
-    @pl.when(pl.program_id(0) == pl.num_programs(0) - 1)
-    def _():
-        for copy in passed:
-            copy.wait()
+        fresh[n] = (acc - recon).astype(BF16)
+        leaving(n).start()
+
+    @pl.loop(0, nblocks // group)
+    def _(g):
+        for b in range(group):
+            product(g * group + b, b)
+            if b:
+                finish(g * group + b - 1, b - 1)
+        finish(g * group + group - 1, group - 1)
+        width = group * sub
+        cols = pl.ds(pl.multiple_of(g * width, width), width)
+        for i in range(ncol // 2):
+            which, to = divmod(place(i, ncol // 2), ncol // 4)
+            z = idx_ref[2] ^ i
+            for whose, refs_of in ((core, code_refs[:2]), (1 - core, code_refs[2:])):
+                at = pl.multiple_of((2 * z + whose) * mine_tokens, mine_tokens)
+                refs_of[which][to * mine_tokens : (to + 1) * mine_tokens, cols] = code_buf[
+                    pl.ds(at, mine_tokens), :
+                ]
+
+    for copy in passed:
+        copy.wait()
+
+    @pl.loop(0, nblocks)
+    def _(n):
+        leaving(n).wait()
 
 
 def compress_call(idx, pieces, weight, feedback, compress, ncol):
@@ -107,33 +127,35 @@
     tokens = feedback.shape[1]
     nblocks = units // blk
     quarter = tokens // 4
-    per = 3 if nblocks % 3 == 0 else 1
+    group = 3 if nblocks % 3 == 0 else 1
     return pl.pallas_call(
-        functools.partial(compress_kernel, nrow, ncol),
+        functools.partial(compress_kernel, nrow, ncol, group),
         grid_spec=pltpu.PrefetchScalarGridSpec(
             num_scalar_prefetch=1,
-            grid=(nblocks // per,),
+            grid=(1,),
             in_specs=[pl.BlockSpec((tokens // nrow, width), lambda j, s: (0, 0))]
             + [pl.BlockSpec(memory_space=pltpu.VMEM)] * (nrow - 1)
-            + [
-                pl.BlockSpec((per * blk, width), lambda j, s: (j, 0)),
-                pl.BlockSpec((1, tokens, per * blk), lambda j, s: (0, 0, j)),
-                pl.BlockSpec((blk, sub), lambda j, s: (0, 0)),
-            ],
-            out_specs=[pl.BlockSpec((1, tokens, per * blk), lambda j, s: (0, 0, j))]
+            + [pl.BlockSpec(memory_space=pl.ANY)] * 2
+            + [pl.BlockSpec((blk, sub), lambda j, s: (0, 0))],
+            out_specs=[pl.BlockSpec(memory_space=pl.ANY)]
             + [pl.BlockSpec(memory_space=pltpu.VMEM)] * 4
             + [pl.BlockSpec(memory_space=pl.ANY)],
             scratch_shapes=[
+                pltpu.VMEM((nblocks, blk, width), BF16),
+                pltpu.VMEM((nblocks, tokens, blk), BF16),
+                pltpu.VMEM((nblocks, tokens, blk), BF16),
                 pltpu.VMEM((tokens, width), BF16),
-                pltpu.VMEM((per, tokens, blk), F32),
-                pltpu.VMEM((tokens, per * sub), BF16),
+                pltpu.VMEM((group, tokens, blk), F32),
+                pltpu.VMEM((tokens, group * sub), BF16),
+                pltpu.SemaphoreType.DMA((2, nblocks)),
+                pltpu.SemaphoreType.DMA((nblocks,)),
                 pltpu.SemaphoreType.DMA((nrow,)),
             ],
         ),
         out_shape=[pltpu.HBM((1, tokens, units), BF16)]
         + [jax.ShapeDtypeStruct((quarter, nblocks * sub), BF16)] * 4
         + [pltpu.HBM((tokens, width), BF16)],
-        compiler_params=pltpu.CompilerParams(vmem_limit_bytes=30 * MIB),
+        compiler_params=pltpu.CompilerParams(vmem_limit_bytes=44 * MIB),
         cost_estimate=LONG,
         name="compress_codes",
     )(idx, *in_hbm(pieces[0]), *pieces[1:], *in_hbm(weight, feedback, compress))
@@ -187,54 +209,53 @@
     )(idx, *in_hbm(hidden))
 
 
-def gw_kernel(npieces, steps, idx_ref, own_ref, diag_ref, swapped_ref, *refs):
+def gw_kernel(npieces, low, block, idx_ref, hidden_hbm, diag_ref, swapped_ref, *refs):
     pieces = refs[:npieces]
-    grads_ref = refs[npieces]
-    out_ref, lhs = refs[-2:]
-    step_tokens, block = own_ref.shape
-    j = pl.program_id(0)
-    core = idx_ref[1]
-
-    def put(slot, x):
-        lhs[slot * step_tokens : (slot + 1) * step_tokens, :] = x
+    grads_hbm = refs[npieces]
+    out_hbm, own, grads, out, in_sems, out_sems = refs[-6:]
+    length = own.shape[1]
+    units = out_hbm.shape[0]
+    steps = length // 2 // block
+    row, core = idx_ref[0], idx_ref[1]
 
     def columns(i):
-        return pl.ds(pl.multiple_of(i * block, block), block)
-
-    put(0, own_ref[...])
-    for i, piece in enumerate(pieces):
-        put(2 + i, piece[:, columns(gw_block(j, core, steps))])
-
-    @pl.when(j < steps)
-    def _():
-        put(1, diag_ref[:, columns(j)])
-
-    @pl.when(j >= steps)
-    def _():
-        put(1, swapped_ref[:, columns(j - steps)])
-
-    out_ref[...] = lax.dot_general(
-        lhs[...], grads_ref[...], (((0,), (0,)), ((), ())), preferred_element_type=F32
-    ).astype(BF16)
-
-
-def gw_block(j, core, steps):
-    return jnp.where(j < steps, core, 1 - core) * steps + lax.rem(j, steps)
+        half = core if i < steps else 1 - core
+        return pl.ds(pl.multiple_of((half * steps + i % steps) * block, block), block)
+
+    source = pl.ds(pl.multiple_of(row * units + low, block), length)
+    arriving = [
+        pltpu.make_async_copy(hidden_hbm.at[:, source], own, in_sems.at[0]),
+        pltpu.make_async_copy(grads_hbm, grads, in_sems.at[1]),
+    ]
+    for copy in arriving:
+        copy.start()
+    for copy in arriving:
+        copy.wait()
+    leaving = []
+    for i in range(2 * steps):
+        from_last = diag_ref if i < steps else swapped_ref
+        at = (i % steps) * block
+        lhs = [own[:, columns(i)], from_last[:, at : at + block]]
+        lhs = jnp.concatenate(lhs + [x[:, columns(i)] for x in pieces], axis=0)
+        out[i] = lax.dot_general(
+            lhs, grads[...], (((0,), (0,)), ((), ())), preferred_element_type=F32
+        ).astype(BF16)
+        to = columns(i)
+        to = pl.ds(pl.multiple_of(low + to.start, block), block)
+        leaving.append(pltpu.make_async_copy(out.at[i], out_hbm.at[to, :], out_sems.at[i]))
+        leaving[-1].start()
+    for copy in leaving:
+        copy.wait()
 
 
 def gw_call(idx, hidden, diag, swapped, pieces, grads, prev, low, units):
     tokens, width = grads.shape
     step_tokens, half = diag.shape
     block = units // GW_BLOCKS
-    steps = half // block
-    at_low = low // block
-
-    def at(j, s):
-        return at_low + gw_block(j, s[1], steps)
-
-    in_specs = [pl.BlockSpec((step_tokens, block), lambda j, s: (0, s[0] * GW_BLOCKS + at(j, s)))]
+    count = 2 * half // block
+    in_specs = [pl.BlockSpec(memory_space=pl.ANY)]
     in_specs += [pl.BlockSpec(memory_space=pltpu.VMEM)] * (2 + len(pieces))
-    in_specs += [pl.BlockSpec((tokens, width), lambda j, s: (0, 0))]
+    in_specs += [pl.BlockSpec(memory_space=pl.ANY)]
     args = [*in_hbm(hidden), diag, swapped, *pieces, *in_hbm(grads)]
     aliases = {}
     if prev is not None:
@@ -242,13 +263,19 @@
         args += [prev]
         aliases = {len(args): 0}
     return pl.pallas_call(
-        functools.partial(gw_kernel, len(pieces), steps),
+        functools.partial(gw_kernel, len(pieces), low, block),
         grid_spec=pltpu.PrefetchScalarGridSpec(
             num_scalar_prefetch=1,
-            grid=(2 * steps,),
+            grid=(1,),
             in_specs=in_specs,
-            out_specs=pl.BlockSpec((block, width), lambda j, s: (at(j, s), 0)),
-            scratch_shapes=[pltpu.VMEM((tokens, block), BF16)],
+            out_specs=pl.BlockSpec(memory_space=pl.ANY),
+            scratch_shapes=[
+                pltpu.VMEM((step_tokens, 2 * half), BF16),
+                pltpu.VMEM((tokens, width), BF16),
+                pltpu.VMEM((count, block, width), BF16),
+                pltpu.SemaphoreType.DMA((2,)),
+                pltpu.SemaphoreType.DMA((count,)),
+            ],
         ),
         out_shape=pltpu.HBM((units, width), BF16),
         input_output_aliases=aliases,
@@ -334,6 +361,7 @@
         swapped = [over_col(x, 1) for x in parts]
         return parts[-1], swapped[-1], [x for pair in zip(parts[:-1], swapped[:-1]) for x in pair]
 
+    packed, grads[1:-1] = after((list(packed), grads[1:-1]))
     early = fetch(packed[: len(pairs) + 1])
     new_feedback, *codes, ordered = compress_call(idx, grads, weight, feedback, compress, ncol)
     late = fetch(packed[len(pairs) + 1 :])

time: 63.7 us -> 65.7 us (1.031)
  waiting for transfers between devices: 13 us -> 15.5 us
  starting transfers between devices: 17.4 us -> 15.5 us
  Pallas kernels: 32 us -> 33.4 us
    ppermute x5, waiting for transfers between devices: 3.69 us -> 5.61 us  [over_row(): return lax.ppermute(x, 'row', xor_perm(nrow, k))]
    ppermute x5, starting transfers between devices: 10.4 us -> 8.92 us  [over_row(): return lax.ppermute(x, 'row', xor_perm(nrow, k))]
    pallas_call x3, Pallas kernels: 26.9 us -> 28.3 us  [the longest x1 16.9 us: compress_call(): pl.pallas_call(functools.partial(compress_kernel, nrow, ncol, group), gri...]
  transfers between devices with their start and end apart: 15 -> 15, of which waited for: 3 -> 5; matrix products, arithmetic and copies ran while one was open for 1% -> 0% of each run, Pallas kernels for 40% -> 42%
where the time goes in v2:
time: 65.7 us; the launch traced here: 65.5 us
  Pallas kernels  33.4 us (51%)
  starting transfers between devices  15.5 us (24%)
  waiting for transfers between devices  15.5 us (24%)
  between operations  0.73 us (1%)
    pallas_call x1, Pallas kernels, compress_call(): pl.pallas_call(functools.partial(compress_kernel, nrow, ncol, group), gri...  16.9 us
    pallas_call x2, Pallas kernels, gw_call(): pl.pallas_call(functools.partial(gw_kernel, len(pieces), low, block), gri...  11.5 us
    ppermute x8, waiting for transfers between devices, over_col(): return lax.ppermute(x, 'col', xor_perm(ncol, k))  9.89 us
    ppermute x5, starting transfers between devices, over_row(): return lax.ppermute(x, 'row', xor_perm(nrow, k))  8.92 us
    ppermute x8, starting transfers between devices, over_col(): return lax.ppermute(x, 'col', xor_perm(ncol, k))  5.94 us
    ppermute x5, waiting for transfers between devices, over_row(): return lax.ppermute(x, 'row', xor_perm(nrow, k))  5.61 us
    pallas_call x1, Pallas kernels, pack_call(): pl.pallas_call(functools.partial(pack_kernel, parts), grid_spec=pltpu.Pre...  3.03 us
    pallas_call x1, Pallas kernels, gi_call(): pl.pallas_call(gi_kernel, grid=(nblocks // per,), in_specs=[spec] * (1 +...  2.05 us
  transfers between devices with their start and end apart: 15, of which 5 were waited for; matrix products, arithmetic and copies ran while one was open for 0% of the time, Pallas kernels for 42%

profile of v2, /device:TPU:0, one launch (start us, length us, event | category | flops | bytes accessed | tf_op | source)
XLA Modules:
  0.0 65.5 jit_solution(838962888013325948)
XLA Ops:
  0.6 3.0 %collective-permute-start.1 = (bf16[128,768]{1,0:T(8,128)(2,1)}, bf16[128,768]{1,0:T(8,128)(2,1)S(1)}, u32[]{:S(2)}, u32[]{:S(2)}) collective-permute-start(bf16[128,768]{1,0:T(8,128)(2,1)} %refs_0_.1), channel_id=1, source_target_pairs={{0,16},{8,24},{16,0},{24,8},{1,17},{9,25},{17,1},{25,9},{2,18},{10... | collective-permute-start | bytes 589832 | tf_op jit(solution)/shard_map/ppermute | solution.py:332
  3.7 1.5 %collective-permute-start = (bf16[128,768]{1,0:T(8,128)(2,1)}, bf16[128,768]{1,0:T(8,128)(2,1)S(1)}, u32[]{:S(2)}, u32[]{:S(2)}) collective-permute-start(bf16[128,768]{1,0:T(8,128)(2,1)} %refs_0_.1), channel_id=1, source_target_pairs={{0,8},{8,0},{16,24},{24,16},{1,9},{9,1},{17,25},{25,17},{2,10},{10... | collective-permute-start | bytes 589832 | tf_op jit(solution)/shard_map/ppermute | solution.py:332
  5.2 0.1 collective-permute-start.4
  5.2 0.1 pad_add_fusion.idx_ref
  5.3 3.0 %pack_hidden.1 = (bf16[128,3072]{1,0:T(8,128)(2,1)}, bf16[128,1536]{1,0:T(8,128)(2,1)}, bf16[128,3072]{1,0:T(8,128)(2,1)}, bf16[128,1536]{1,0:T(8,128)(2,1)}) custom-call(s32[3]{0:T(128)S(1)} %pad_add_fusion.idx_ref, bf16[128,24576]{1,0:T(8,128)(2,1)} %hidden_hbm.3), custom_call_target="tpu_custom_call" | custom-call | flops 1 | bytes 1 | tf_op jit(solution)/shard_map/pack_hidden/pallas_call | solution.py:193
  8.3 0.5 collective-permute-done.1.refs_2_
  8.8 2.9 %collective-permute-done.refs_1_ = bf16[128,768]{1,0:T(8,128)(2,1)S(1)} collective-permute-done((bf16[128,768]{1,0:T(8,128)(2,1)}, bf16[128,768]{1,0:T(8,128)(2,1)S(1)}, u32[]{:S(2)}, u32[]{:S(2)}) %collective-permute-start) | collective-permute-done | bytes 196640 | tf_op jit(solution)/shard_map/ppermute | solution.py:332
  11.7 1.4 %collective-permute-start.3 = (bf16[128,1536]{1,0:T(8,128)(2,1)}, bf16[128,1536]{1,0:T(8,128)(2,1)S(1)}, u32[]{:S(2)}, u32[]{:S(2)}) collective-permute-start(bf16[128,1536]{1,0:T(8,128)(2,1)} %get-tuple-element.36), channel_id=1, source_target_pairs={{0,24},{8,16},{16,8},{24,0},{1,25},{9,17},{17,9},{25,1},{2,26},{10... | collective-permute-start | bytes 1179656 | tf_op jit(solution)/shard_map/ppermute | solution.py:332
  13.1 0.1 collective-permute-start.2
  13.3 2.2 %collective-permute-done.4.refs_3_ = bf16[128,768]{1,0:T(8,128)(2,1)S(1)} collective-permute-done((bf16[128,768]{1,0:T(8,128)(2,1)}, bf16[128,768]{1,0:T(8,128)(2,1)S(1)}, u32[]{:S(2)}, u32[]{:S(2)}) %collective-permute-start.4) | collective-permute-done | bytes 196640 | tf_op jit(solution)/shard_map/ppermute | solution.py:332
  15.5 16.9 %compress_codes.1 = (bf16[1,512,6144]{2,1,0:T(8,128)(2,1)}, bf16[128,1536]{1,0:T(8,128)(2,1)S(1)}, bf16[128,1536]{1,0:T(8,128)(2,1)S(1)}, bf16[128,1536]{1,0:T(8...) custom-call(s32[3]{0:T(128)S(1)} %pad_add_fusion.idx_ref, bf16[128,768]{1,0:T(8,128)(2,1)} %refs_0_.1, ...), custom_call_target="tpu_custom_call" | custom-call | flops 68719476736 | bytes 268435456 | tf_op jit(solution)/shard_map/compress_codes/pallas_call | solution.py:131
  32.4 0.1 collective-permute-start.5
  32.4 0.5 collective-permute-start.6
  32.9 2.9 %collective-permute-start.11 = (bf16[128,1536]{1,0:T(8,128)(2,1)S(1)}, bf16[128,1536]{1,0:T(8,128)(2,1)S(1)}, u32[]{:S(2)}, u32[]{:S(2)}) collective-permute-start(bf16[128,1536]{1,0:T(8,128)(2,1)S(1)} %copy-done.2), channel_id=1, source_target_pairs={{0,24},{8,16},{16,8},{24,0},{1,25},{9,17},{17,9},{25,1},{2,26},{10... | collective-permute-start | bytes 1179656 | tf_op jit(solution)/shard_map/ppermute | solution.py:332
  35.9 0.5 collective-permute-start.10
  36.4 0.0 collective-permute-done.5
  36.4 0.0 collective-permute-done.6
  36.4 0.0 collective-permute-done.2.refs_0_
  36.4 0.1 add_convert_fusion
  36.5 1.6 %collective-permute-start.9 = (bf16[128,1536]{1,0:T(8,128)(2,1)S(1)}, bf16[128,1536]{1,0:T(8,128)(2,1)S(1)}, u32[]{:S(2)}, u32[]{:S(2)}) collective-permute-start(bf16[128,1536]{1,0:T(8,128)(2,1)S(1)} %add_convert_fusion), channel_id=1, source_target_pairs={{0,2},{1,3},{2,0},{3,1},{4,6},{5,7},{6,4},{7,5},{8,10},{9,11},{10,... | collective-permute-start | bytes 1179656 | tf_op jit(solution)/shard_map/ppermute | solution.py:335
  38.2 0.0 collective-permute-start.7
  38.2 0.5 collective-permute-start.8
  38.7 0.1 convert_add_fusion
  38.8 8.3 %collective-permute-done.9 = bf16[128,1536]{1,0:T(8,128)(2,1)S(1)} collective-permute-done((bf16[128,1536]{1,0:T(8,128)(2,1)S(1)}, bf16[128,1536]{1,0:T(8,128)(2,1)S(1)}, u32[]{:S(2)}, u32[]{:S(2)}) %collective-permute-start.9) | collective-permute-done | bytes 393248 | tf_op jit(solution)/shard_map/ppermute | solution.py:335
  47.1 0.1 fusion
  47.2 2.7 %collective-permute-start.12 = (bf16[64,1536]{1,0:T(8,128)(2,1)S(1)}, bf16[64,1536]{1,0:T(8,128)(2,1)S(1)}, u32[]{:S(2)}, u32[]{:S(2)}) collective-permute-start(bf16[64,1536]{1,0:T(8,128)(2,1)S(1)} %get-tuple-element.59), channel_id=1, source_target_pairs={{0,4},{1,5},{2,6},{3,7},{4,0},{5,1},{6,2},{7,3},{8,12},{9,13},{10,... | collective-permute-start | bytes 589832 | tf_op jit(solution)/shard_map/ppermute | solution.py:335
  49.8 5.7 %weight_gradient.2.refs_3_ = bf16[6144,768]{1,0:T(8,128)(2,1)} custom-call(s32[3]{0:T(128)S(1)} %pad_add_fusion.idx_ref, bf16[128,24576]{1,0:T(8,128)(2,1)} %hidden_hbm.3, bf16[128,1536]{1,0:T(8,128)(2,1)S(1)} %collective-permute-done.3.diag_ref, bf16[128,1536]{1,0:T(8,128)(2,1)S(1)} %collective-permute-done.7.swapped_ref, ...), custom_call_target="tpu_custom_call" | custom-call | flops 1 | bytes 1 | tf_op jit(solution)/shard_map/weight_gradient/pallas_call | solution.py:265
  55.6 0.1 collective-permute-start.13
  55.7 0.5 collective-permute-start.14
  56.2 1.5 %collective-permute-done.12.refs_0_ = bf16[64,1536]{1,0:T(8,128)(2,1)S(1)} collective-permute-done((bf16[64,1536]{1,0:T(8,128)(2,1)S(1)}, bf16[64,1536]{1,0:T(8,128)(2,1)S(1)}, u32[]{:S(2)}, u32[]{:S(2)}) %collective-permute-start.12) | collective-permute-done | bytes 196640 | tf_op jit(solution)/shard_map/ppermute | solution.py:335
  57.7 2.0 %grad_input.1 = bf16[64,6144]{1,0:T(8,128)(2,1)} custom-call(f32[64,1536]{1,0:T(8,128)S(1)} %get-tuple-element.50.own_ref, bf16[64,1536]{1,0:T(8,128)(2,1)S(1)} %collective-permute-done.12.refs_0_, bf16[512,128]{1,0:T(8,128)(2,1)S(1)} %copy-done), custom_call_target="tpu_custom_call" | custom-call | flops 68719476736 | bytes 268435456 | tf_op jit(solution)/shard_map/grad_input/pallas_call | solution.py:311
  59.8 5.7 %weight_gradient.3 = bf16[6144,768]{1,0:T(8,128)(2,1)} custom-call(s32[3]{0:T(128)S(1)} %pad_add_fusion.idx_ref, bf16[128,24576]{1,0:T(8,128)(2,1)} %hidden_hbm.3, bf16[128,1536]{1,0:T(8,128)(2,1)S(1)} %collective-permute-done.11.diag_ref, bf16[128,1536]{1,0:T(8,128)(2,1)S(1)} %collective-permute-done.13.swapped_ref, ...), custom_call_target="tpu_custom_call", output_to_operand_aliasing={{}: (7, {})} | custom-call | flops 1 | bytes 1 | tf_op jit(solution)/shard_map/weight_gradient/pallas_call | solution.py:265
  (13 shorter events, 0.0 us)
Async XLA Ops:
  0.6 8.1 %collective-permute-start.1 = (bf16[128,768]{1,0:T(8,128)(2,1)}, bf16[128,768]{1,0:T(8,128)(2,1)S(1)}, u32[]{:S(2)}, u32[]{:S(2)}) collective-permute-start(bf16[128,768]{1,0:T(8,128)(2,1)} %refs_0_.1), channel_id=1, source_target_pairs={{0,16},{8,24},{16,0},{24,8},{1,17},{9,25},{17,1},{25,9},{2,18},{10... | collective-permute-start | bytes 589832 | tf_op jit(solution)/shard_map/ppermute | solution.py:332
  3.7 8.0 %collective-permute-start = (bf16[128,768]{1,0:T(8,128)(2,1)}, bf16[128,768]{1,0:T(8,128)(2,1)S(1)}, u32[]{:S(2)}, u32[]{:S(2)}) collective-permute-start(bf16[128,768]{1,0:T(8,128)(2,1)} %refs_0_.1), channel_id=1, source_target_pairs={{0,8},{8,0},{16,24},{24,16},{1,9},{9,1},{17,25},{25,17},{2,10},{10... | collective-permute-start | bytes 589832 | tf_op jit(solution)/shard_map/ppermute | solution.py:332
  5.2 10.3 %collective-permute-start.4 = (bf16[128,768]{1,0:T(8,128)(2,1)}, bf16[128,768]{1,0:T(8,128)(2,1)S(1)}, u32[]{:S(2)}, u32[]{:S(2)}) collective-permute-start(bf16[128,768]{1,0:T(8,128)(2,1)} %refs_0_.1), channel_id=1, source_target_pairs={{0,24},{8,16},{16,8},{24,0},{1,25},{9,17},{17,9},{25,1},{2,26},{10... | collective-permute-start | bytes 589832 | tf_op jit(solution)/shard_map/ppermute | solution.py:332
  11.7 21.2 %copy-start.2 = (bf16[128,1536]{1,0:T(8,128)(2,1)S(1)}, bf16[128,1536]{1,0:T(8,128)(2,1)}, u32[]{:S(2)}) copy-start(bf16[128,1536]{1,0:T(8,128)(2,1)} %get-tuple-element.49) | copy-start | bytes 1179652
  11.7 24.2 %copy-start.1 = (bf16[128,3072]{1,0:T(8,128)(2,1)S(1)}, bf16[128,3072]{1,0:T(8,128)(2,1)}, u32[]{:S(2)}) copy-start(bf16[128,3072]{1,0:T(8,128)(2,1)} %get-tuple-element.48) | copy-start | bytes 2359300
  11.7 24.2 %collective-permute-start.3 = (bf16[128,1536]{1,0:T(8,128)(2,1)}, bf16[128,1536]{1,0:T(8,128)(2,1)S(1)}, u32[]{:S(2)}, u32[]{:S(2)}) collective-permute-start(bf16[128,1536]{1,0:T(8,128)(2,1)} %get-tuple-element.36), channel_id=1, source_target_pairs={{0,24},{8,16},{16,8},{24,0},{1,25},{9,17},{17,9},{25,1},{2,26},{10... | collective-permute-start | bytes 1179656 | tf_op jit(solution)/shard_map/ppermute | solution.py:332
  13.1 23.3 %collective-permute-start.2 = (bf16[128,3072]{1,0:T(8,128)(2,1)}, bf16[128,3072]{1,0:T(8,128)(2,1)S(1)}, u32[]{:S(2)}, u32[]{:S(2)}) collective-permute-start(bf16[128,3072]{1,0:T(8,128)(2,1)} %get-tuple-element.35), channel_id=1, source_target_pairs={{0,8},{1,17},{2,10},{3,19},{4,12},{5,21},{6,14},{7,23},{8,0},{9,25... | collective-permute-start | bytes 2359304 | tf_op jit(solution)/shard_map/ppermute | solution.py:357
  32.4 4.0 %collective-permute-start.5 = (bf16[128,1536]{1,0:T(8,128)(2,1)S(1)}, bf16[128,1536]{1,0:T(8,128)(2,1)S(1)}, u32[]{:S(2)}, u32[]{:S(2)}) collective-permute-start(bf16[128,1536]{1,0:T(8,128)(2,1)S(1)} %get-tuple-element.39), channel_id=1, source_target_pairs={{0,1},{1,0},{2,3},{3,2},{4,5},{5,4},{6,7},{7,6},{8,9},{9,8},{10,11... | collective-permute-start | bytes 1179656 | tf_op jit(solution)/shard_map/ppermute | solution.py:335
  32.4 4.0 %collective-permute-start.6 = (bf16[128,1536]{1,0:T(8,128)(2,1)S(1)}, bf16[128,1536]{1,0:T(8,128)(2,1)S(1)}, u32[]{:S(2)}, u32[]{:S(2)}) collective-permute-start(bf16[128,1536]{1,0:T(8,128)(2,1)S(1)} %get-tuple-element.40), channel_id=1, source_target_pairs={{0,1},{1,0},{2,3},{3,2},{4,5},{5,4},{6,7},{7,6},{8,9},{9,8},{10,11... | collective-permute-start | bytes 1179656 | tf_op jit(solution)/shard_map/ppermute | solution.py:335
  32.9 22.6 %collective-permute-start.11 = (bf16[128,1536]{1,0:T(8,128)(2,1)S(1)}, bf16[128,1536]{1,0:T(8,128)(2,1)S(1)}, u32[]{:S(2)}, u32[]{:S(2)}) collective-permute-start(bf16[128,1536]{1,0:T(8,128)(2,1)S(1)} %copy-done.2), channel_id=1, source_target_pairs={{0,24},{8,16},{16,8},{24,0},{1,25},{9,17},{17,9},{25,1},{2,26},{10... | collective-permute-start | bytes 1179656 | tf_op jit(solution)/shard_map/ppermute | solution.py:332
  35.9 19.7 %collective-permute-start.10 = (bf16[128,3072]{1,0:T(8,128)(2,1)S(1)}, bf16[128,3072]{1,0:T(8,128)(2,1)S(1)}, u32[]{:S(2)}, u32[]{:S(2)}) collective-permute-start(bf16[128,3072]{1,0:T(8,128)(2,1)S(1)} %copy-done.1), channel_id=1, source_target_pairs={{0,8},{1,17},{2,10},{3,19},{4,12},{5,21},{6,14},{7,23},{8,0},{9,25... | collective-permute-start | bytes 2359304 | tf_op jit(solution)/shard_map/ppermute | solution.py:357
  36.5 10.6 %collective-permute-start.9 = (bf16[128,1536]{1,0:T(8,128)(2,1)S(1)}, bf16[128,1536]{1,0:T(8,128)(2,1)S(1)}, u32[]{:S(2)}, u32[]{:S(2)}) collective-permute-start(bf16[128,1536]{1,0:T(8,128)(2,1)S(1)} %add_convert_fusion), channel_id=1, source_target_pairs={{0,2},{1,3},{2,0},{3,1},{4,6},{5,7},{6,4},{7,5},{8,10},{9,11},{10,... | collective-permute-start | bytes 1179656 | tf_op jit(solution)/shard_map/ppermute | solution.py:335
  38.2 11.7 %collective-permute-start.7 = (bf16[128,1536]{1,0:T(8,128)(2,1)S(1)}, bf16[128,1536]{1,0:T(8,128)(2,1)S(1)}, u32[]{:S(2)}, u32[]{:S(2)}) collective-permute-start(bf16[128,1536]{1,0:T(8,128)(2,1)S(1)} %collective-permute-done.3.diag_ref), channel_id=1, source_target_pairs={{0,1},{1,0},{2,3},{3,2},{4,5},{5,4},{6,7},{7,6},{8,9},{9,8},{10,11... | collective-permute-start | bytes 1179656 | tf_op jit(solution)/shard_map/ppermute | solution.py:335
  38.2 11.7 %collective-permute-start.8 = (bf16[128,3072]{1,0:T(8,128)(2,1)S(1)}, bf16[128,3072]{1,0:T(8,128)(2,1)S(1)}, u32[]{:S(2)}, u32[]{:S(2)}) collective-permute-start(bf16[128,3072]{1,0:T(8,128)(2,1)S(1)} %collective-permute-done.2.refs_0_), channel_id=1, source_target_pairs={{0,1},{1,0},{2,3},{3,2},{4,5},{5,4},{6,7},{7,6},{8,9},{9,8},{10,11... | collective-permute-start | bytes 2359304 | tf_op jit(solution)/shard_map/ppermute | solution.py:335
  47.2 10.5 %collective-permute-start.12 = (bf16[64,1536]{1,0:T(8,128)(2,1)S(1)}, bf16[64,1536]{1,0:T(8,128)(2,1)S(1)}, u32[]{:S(2)}, u32[]{:S(2)}) collective-permute-start(bf16[64,1536]{1,0:T(8,128)(2,1)S(1)} %get-tuple-element.59), channel_id=1, source_target_pairs={{0,4},{1,5},{2,6},{3,7},{4,0},{5,1},{6,2},{7,3},{8,12},{9,13},{10,... | collective-permute-start | bytes 589832 | tf_op jit(solution)/shard_map/ppermute | solution.py:335
  49.8 7.9 %copy-start = (bf16[512,128]{1,0:T(8,128)(2,1)S(1)}, bf16[512,128]{1,0:T(8,128)(2,1)}, u32[]{:S(2)}) copy-start(bf16[512,128]{1,0:T(8,128)(2,1)} %refs_1_.1) | copy-start | bytes 393220
  55.6 4.2 %collective-permute-start.13 = (bf16[128,1536]{1,0:T(8,128)(2,1)S(1)}, bf16[128,1536]{1,0:T(8,128)(2,1)S(1)}, u32[]{:S(2)}, u32[]{:S(2)}) collective-permute-start(bf16[128,1536]{1,0:T(8,128)(2,1)S(1)} %collective-permute-done.11.diag_ref), channel_id=1, source_target_pairs={{0,1},{1,0},{2,3},{3,2},{4,5},{5,4},{6,7},{7,6},{8,9},{9,8},{10,11... | collective-permute-start | bytes 1179656 | tf_op jit(solution)/shard_map/ppermute | solution.py:335
  55.7 4.1 %collective-permute-start.14 = (bf16[128,3072]{1,0:T(8,128)(2,1)S(1)}, bf16[128,3072]{1,0:T(8,128)(2,1)S(1)}, u32[]{:S(2)}, u32[]{:S(2)}) collective-permute-start(bf16[128,3072]{1,0:T(8,128)(2,1)S(1)} %collective-permute-done.10.refs_0_), channel_id=1, source_target_pairs={{0,1},{1,0},{2,3},{3,2},{4,5},{5,4},{6,7},{7,6},{8,9},{9,8},{10,11... | collective-permute-start | bytes 2359304 | tf_op jit(solution)/shard_map/ppermute | solution.py:335

commit v3 on v1

--- a/solution.py
+++ b/solution.py
@@ -10,7 +10,7 @@
 F32 = jnp.float32
 BF16 = jnp.bfloat16
 MIB = 1024 * 1024
-GW_BLOCKS = 4
+GW_BLOCKS = 12
 LONG = pl.CostEstimate(flops=1 << 36, bytes_accessed=1 << 28, transcendentals=0)
 COST = pl.CostEstimate(flops=1, bytes_accessed=1, transcendentals=0)
 
@@ -59,28 +59,33 @@
         for k in range(nrow):
             grads[rows_at(row ^ k), :] = pieces[k][...]
 
-    def product(b):
-        cols = slice(b * blk, (b + 1) * blk)
+    tokens = grads.shape[0]
+
+    def product(b, part):
+        cols = slice(part * blk // 2, (part + 1) * blk // 2)
+        units = slice(b * blk + cols.start, b * blk + cols.stop)
         partial = lax.dot_general(
-            grads[...], weight_ref[cols, :], (((1,), (1,)), ((), ())), preferred_element_type=F32
+            grads[...], weight_ref[units, :], (((1,), (1,)), ((), ())), preferred_element_type=F32
         )
-        acc_buf[b] = partial + feedback_ref[0, :, cols].astype(F32)
-
-    def finish(b):
-        acc = acc_buf[b]
+        acc_buf[b, :, cols] = partial + feedback_ref[0, :, units].astype(F32)
+
+    def finish(b, part):
+        rows = slice(part * tokens // 2, (part + 1) * tokens // 2)
+        acc = acc_buf[b, rows]
         code = jnp.dot(acc.astype(BF16), compress_ref[...], preferred_element_type=F32)
         code_low = code.astype(BF16)
-        code_buf[:, b * sub : (b + 1) * sub] = code_low
+        code_buf[rows, b * sub : (b + 1) * sub] = code_low
         recon = lax.dot_general(
             code_low, compress_ref[...], (((1,), (1,)), ((), ())), preferred_element_type=F32
         )
-        fresh_ref[0, :, b * blk : (b + 1) * blk] = (acc - recon).astype(BF16)
-
-    for b in range(count):
-        product(b)
-        if b:
-            finish(b - 1)
-    finish(count - 1)
+        fresh_ref[0, rows, b * blk : (b + 1) * blk] = (acc - recon).astype(BF16)
+
+    for b in range(count + 1):
+        for part in range(2):
+            if b < count:
+                product(b, part)
+            if b:
+                finish(b - 1, part)
 
     mine_tokens = grads.shape[0] // ncol
     width = count * sub
@@ -187,54 +192,53 @@
     )(idx, *in_hbm(hidden))
 
 
-def gw_kernel(npieces, steps, idx_ref, own_ref, diag_ref, swapped_ref, *refs):
+def gw_kernel(npieces, low, block, idx_ref, hidden_hbm, diag_ref, swapped_ref, *refs):
     pieces = refs[:npieces]
-    grads_ref = refs[npieces]
-    out_ref, lhs = refs[-2:]
-    step_tokens, block = own_ref.shape
-    j = pl.program_id(0)
-    core = idx_ref[1]
-
-    def put(slot, x):
-        lhs[slot * step_tokens : (slot + 1) * step_tokens, :] = x
+    grads_hbm = refs[npieces]
+    out_hbm, own, grads, out, in_sems, out_sems = refs[-6:]
+    length = own.shape[1]
+    units = out_hbm.shape[0]
+    steps = length // 2 // block
+    row, core = idx_ref[0], idx_ref[1]
 
     def columns(i):
-        return pl.ds(pl.multiple_of(i * block, block), block)
-
-    put(0, own_ref[...])
-    for i, piece in enumerate(pieces):
-        put(2 + i, piece[:, columns(gw_block(j, core, steps))])
-
-    @pl.when(j < steps)
-    def _():
-        put(1, diag_ref[:, columns(j)])
-
-    @pl.when(j >= steps)
-    def _():
-        put(1, swapped_ref[:, columns(j - steps)])
-
-    out_ref[...] = lax.dot_general(
-        lhs[...], grads_ref[...], (((0,), (0,)), ((), ())), preferred_element_type=F32
-    ).astype(BF16)
-
-
-def gw_block(j, core, steps):
-    return jnp.where(j < steps, core, 1 - core) * steps + lax.rem(j, steps)
+        half = core if i < steps else 1 - core
+        return pl.ds(pl.multiple_of((half * steps + i % steps) * block, block), block)
+
+    source = pl.ds(pl.multiple_of(row * units + low, block), length)
+    arriving = [
+        pltpu.make_async_copy(hidden_hbm.at[:, source], own, in_sems.at[0]),
+        pltpu.make_async_copy(grads_hbm, grads, in_sems.at[1]),
+    ]
+    for copy in arriving:
+        copy.start()
+    for copy in arriving:
+        copy.wait()
+    leaving = []
+    for i in range(2 * steps):
+        from_last = diag_ref if i < steps else swapped_ref
+        at = (i % steps) * block
+        lhs = [own[:, columns(i)], from_last[:, at : at + block]]
+        lhs = jnp.concatenate(lhs + [x[:, columns(i)] for x in pieces], axis=0)
+        out[i] = lax.dot_general(
+            lhs, grads[...], (((0,), (0,)), ((), ())), preferred_element_type=F32
+        ).astype(BF16)
+        to = columns(i)
+        to = pl.ds(pl.multiple_of(low + to.start, block), block)
+        leaving.append(pltpu.make_async_copy(out.at[i], out_hbm.at[to, :], out_sems.at[i]))
+        leaving[-1].start()
+    for copy in leaving:
+        copy.wait()
 
 
 def gw_call(idx, hidden, diag, swapped, pieces, grads, prev, low, units):
     tokens, width = grads.shape
     step_tokens, half = diag.shape
     block = units // GW_BLOCKS
-    steps = half // block
-    at_low = low // block
-
-    def at(j, s):
-        return at_low + gw_block(j, s[1], steps)
-
-    in_specs = [pl.BlockSpec((step_tokens, block), lambda j, s: (0, s[0] * GW_BLOCKS + at(j, s)))]
+    count = 2 * half // block
+    in_specs = [pl.BlockSpec(memory_space=pl.ANY)]
     in_specs += [pl.BlockSpec(memory_space=pltpu.VMEM)] * (2 + len(pieces))
-    in_specs += [pl.BlockSpec((tokens, width), lambda j, s: (0, 0))]
+    in_specs += [pl.BlockSpec(memory_space=pl.ANY)]
     args = [*in_hbm(hidden), diag, swapped, *pieces, *in_hbm(grads)]
     aliases = {}
     if prev is not None:
@@ -242,13 +246,19 @@
         args += [prev]
         aliases = {len(args): 0}
     return pl.pallas_call(
-        functools.partial(gw_kernel, len(pieces), steps),
+        functools.partial(gw_kernel, len(pieces), low, block),
         grid_spec=pltpu.PrefetchScalarGridSpec(
             num_scalar_prefetch=1,
-            grid=(2 * steps,),
+            grid=(1,),
             in_specs=in_specs,
-            out_specs=pl.BlockSpec((block, width), lambda j, s: (at(j, s), 0)),
-            scratch_shapes=[pltpu.VMEM((tokens, block), BF16)],
+            out_specs=pl.BlockSpec(memory_space=pl.ANY),
+            scratch_shapes=[
+                pltpu.VMEM((step_tokens, 2 * half), BF16),
+                pltpu.VMEM((tokens, width), BF16),
+                pltpu.VMEM((count, block, width), BF16),
+                pltpu.SemaphoreType.DMA((2,)),
+                pltpu.SemaphoreType.DMA((count,)),
+            ],
         ),
         out_shape=pltpu.HBM((units, width), BF16),
         input_output_aliases=aliases,
@@ -258,39 +268,33 @@
     )(idx, *args)
 
 
-def gi_kernel(own_ref, *refs):
-    recv = refs[:-2]
+def gi_kernel(parts, *refs):
     compress_ref, out_ref = refs[-2:]
-    total = own_ref[...]
-    for piece in recv:
-        total = total + piece[...].astype(F32)
-    low = total.astype(BF16)
     blk, sub = compress_ref.shape
-    for n in range(low.shape[1] // sub):
-        out_ref[:, n * blk : (n + 1) * blk] = lax.dot_general(
-            low[:, n * sub : (n + 1) * sub],
-            compress_ref[...],
-            (((1,), (1,)), ((), ())),
-            preferred_element_type=F32,
-        ).astype(BF16)
-
-
-def gi_call(own, recv, compress, units):
-    tokens, codes = own.shape
-    blk, sub = compress.shape
-    nblocks = codes // sub
-    per = nblocks // 3 if nblocks % 3 == 0 else 1
-    spec = pl.BlockSpec((tokens, per * sub), lambda j: (0, j))
+    at = 0
+    for own, received in zip(refs[:parts], refs[parts : 2 * parts]):
+        low = (own[...] + received[...].astype(F32)).astype(BF16)
+        for n in range(low.shape[1] // sub):
+            out_ref[:, at : at + blk] = lax.dot_general(
+                low[:, n * sub : (n + 1) * sub],
+                compress_ref[...],
+                (((1,), (1,)), ((), ())),
+                preferred_element_type=F32,
+            ).astype(BF16)
+            at += blk
+
+
+def gi_call(own, received, compress, units):
+    tokens = own[0].shape[0]
     return pl.pallas_call(
-        gi_kernel,
-        grid=(nblocks // per,),
-        in_specs=[spec] * (1 + len(recv)) + [pl.BlockSpec((blk, sub), lambda j: (0, 0))],
-        out_specs=pl.BlockSpec((tokens, per * blk), lambda j: (0, j)),
-        out_shape=pltpu.HBM((tokens, units), BF16),
+        functools.partial(gi_kernel, len(own)),
+        in_specs=[pl.BlockSpec(memory_space=pltpu.VMEM)] * (2 * len(own) + 1),
+        out_specs=pl.BlockSpec(memory_space=pltpu.VMEM),
+        out_shape=jax.ShapeDtypeStruct((tokens, units), BF16),
         compiler_params=pltpu.CompilerParams(vmem_limit_bytes=10 * MIB),
         cost_estimate=LONG,
         name="grad_input",
-    )(own, *recv, compress)
+    )(*own, *received, compress)
 
 
 def on_device(nrow, ncol, out_grad, hidden, weight, compress, feedback):
@@ -339,7 +343,7 @@
     late = fetch(packed[len(pairs) + 1 :])
 
     *others, kept, send = after((*early, *[over_col(x, 1) for x in codes[2:]]))
-    early = swap(others)
+    early = list(swap(others))
     kept, send = [x.astype(F32) + y.astype(F32) for x, y in zip(codes[:2], (kept, send))]
     step = 1
     while True:
@@ -353,7 +357,7 @@
 
     grad_weight = gw_call(idx, hidden, *early, ordered, None, lows[0], units)
     grad_weight, kept, *late = after((grad_weight, kept, *late))
-    grad_input = gi_call(kept, [received], compress, units)
+    grad_input = gi_call([kept], [received], compress, units)
     diag, swapped, pieces = swap(late)
     grad_input, swapped, *pieces = after((grad_input, swapped, *pieces))
     grad_weight = gw_call(idx, hidden, diag, swapped, pieces, ordered, grad_weight, lows[1], units)

time: 63.7 us -> 62.5 us (0.981)
  Pallas kernels: 32 us -> 30.1 us
  waiting for transfers between devices: 13 us -> 13.7 us
    pallas_call x3, Pallas kernels: 14.8 us -> 12.7 us  [the longest x2 11.2 us: gw_call(): pl.pallas_call(functools.partial(gw_kernel, len(pieces), low, block), gri...]
    ppermute x8, waiting for transfers between devices: 9.3 us -> 10 us  [over_col(): return lax.ppermute(x, 'col', xor_perm(ncol, k))]
  transfers between devices with their start and end apart: 15 -> 15, of which waited for: 3 -> 3; matrix products, arithmetic and copies ran while one was open for 1% -> 1% of each run, Pallas kernels for 40% -> 39%
where the time goes in v3:
time: 62.5 us; the launch traced here: 62.3 us
  Pallas kernels  30.1 us (48%)
  starting transfers between devices  17.4 us (28%)
  waiting for transfers between devices  13.7 us (22%)
  between operations  0.73 us (1%)
    pallas_call x1, Pallas kernels, compress_call(): pl.pallas_call(functools.partial(compress_kernel, nrow, ncol), grid_spec=...  14.3 us
    pallas_call x2, Pallas kernels, gw_call(): pl.pallas_call(functools.partial(gw_kernel, len(pieces), low, block), gri...  11.2 us
    ppermute x5, starting transfers between devices, over_row(): return lax.ppermute(x, 'row', xor_perm(nrow, k))  10.4 us
    ppermute x8, waiting for transfers between devices, over_col(): return lax.ppermute(x, 'col', xor_perm(ncol, k))  10 us
    ppermute x8, starting transfers between devices, over_col(): return lax.ppermute(x, 'col', xor_perm(ncol, k))  5.94 us
    ppermute x5, waiting for transfers between devices, over_row(): return lax.ppermute(x, 'row', xor_perm(nrow, k))  3.69 us
    pallas_call x1, Pallas kernels, pack_call(): pl.pallas_call(functools.partial(pack_kernel, parts), grid_spec=pltpu.Pre...  3.03 us
    pallas_call x1, Pallas kernels, gi_call(): pl.pallas_call(functools.partial(gi_kernel, len(own)), in_specs=[pl.Block...  1.54 us
  transfers between devices with their start and end apart: 15, of which 3 were waited for; matrix products, arithmetic and copies ran while one was open for 1% of the time, Pallas kernels for 39%

profile of v3, /device:TPU:0, one launch (start us, length us, event | category | flops | bytes accessed | tf_op | source)
XLA Modules:
  0.0 62.3 jit_solution(3922065844408899144)
XLA Ops:
  0.6 3.0 %collective-permute-start.3 = (bf16[128,768]{1,0:T(8,128)(2,1)}, bf16[128,768]{1,0:T(8,128)(2,1)S(1)}, u32[]{:S(2)}, u32[]{:S(2)}) collective-permute-start(bf16[128,768]{1,0:T(8,128)(2,1)} %refs_0_.1), channel_id=1, source_target_pairs={{0,16},{8,24},{16,0},{24,8},{1,17},{9,25},{17,1},{25,9},{2,18},{10... | collective-permute-start | bytes 589832 | tf_op jit(solution)/shard_map/ppermute | solution.py:309
  3.7 1.5 %collective-permute-start.2 = (bf16[128,768]{1,0:T(8,128)(2,1)}, bf16[128,768]{1,0:T(8,128)(2,1)S(1)}, u32[]{:S(2)}, u32[]{:S(2)}) collective-permute-start(bf16[128,768]{1,0:T(8,128)(2,1)} %refs_0_.1), channel_id=1, source_target_pairs={{0,8},{8,0},{16,24},{24,16},{1,9},{9,1},{17,25},{25,17},{2,10},{10... | collective-permute-start | bytes 589832 | tf_op jit(solution)/shard_map/ppermute | solution.py:309
  5.2 0.1 collective-permute-start.4
  5.2 0.1 pad_add_fusion.idx_ref
  5.3 3.0 %pack_hidden.1 = (bf16[128,3072]{1,0:T(8,128)(2,1)}, bf16[128,1536]{1,0:T(8,128)(2,1)}, bf16[128,3072]{1,0:T(8,128)(2,1)}, bf16[128,1536]{1,0:T(8,128)(2,1)}) custom-call(s32[3]{0:T(128)S(1)} %pad_add_fusion.idx_ref, bf16[128,24576]{1,0:T(8,128)(2,1)} %hidden_hbm.3), custom_call_target="tpu_custom_call" | custom-call | flops 1 | bytes 1 | tf_op jit(solution)/shard_map/pack_hidden/pallas_call | solution.py:176
  8.3 2.9 %collective-permute-start.1 = (bf16[128,1536]{1,0:T(8,128)(2,1)}, bf16[128,1536]{1,0:T(8,128)(2,1)S(1)}, u32[]{:S(2)}, u32[]{:S(2)}) collective-permute-start(bf16[128,1536]{1,0:T(8,128)(2,1)} %get-tuple-element.26), channel_id=1, source_target_pairs={{0,24},{8,16},{16,8},{24,0},{1,25},{9,17},{17,9},{25,1},{2,26},{10... | collective-permute-start | bytes 1179656 | tf_op jit(solution)/shard_map/ppermute | solution.py:309
  11.3 0.5 collective-permute-start
  11.8 3.7 %collective-permute-done.4.refs_3_ = bf16[128,768]{1,0:T(8,128)(2,1)S(1)} collective-permute-done((bf16[128,768]{1,0:T(8,128)(2,1)}, bf16[128,768]{1,0:T(8,128)(2,1)S(1)}, u32[]{:S(2)}, u32[]{:S(2)}) %collective-permute-start.4) | collective-permute-done | bytes 196640 | tf_op jit(solution)/shard_map/ppermute | solution.py:309
  15.5 14.3 %compress_codes.1 = (bf16[1,512,6144]{2,1,0:T(8,128)(2,1)}, bf16[128,1536]{1,0:T(8,128)(2,1)S(1)}, bf16[128,1536]{1,0:T(8,128)(2,1)S(1)}, bf16[128,1536]{1,0:T(8...) custom-call(s32[3]{0:T(128)S(1)} %pad_add_fusion.idx_ref, bf16[128,768]{1,0:T(8,128)(2,1)} %refs_0_.1, ...), custom_call_target="tpu_custom_call" | custom-call | flops 68719476736 | bytes 268435456 | tf_op jit(solution)/shard_map/compress_codes/pallas_call | solution.py:116
  29.8 0.1 collective-permute-start.5
  29.9 0.5 collective-permute-start.6
  30.4 2.9 %collective-permute-start.11 = (bf16[128,1536]{1,0:T(8,128)(2,1)S(1)}, bf16[128,1536]{1,0:T(8,128)(2,1)S(1)}, u32[]{:S(2)}, u32[]{:S(2)}) collective-permute-start(bf16[128,1536]{1,0:T(8,128)(2,1)S(1)} %copy-done.2), channel_id=1, source_target_pairs={{0,24},{8,16},{16,8},{24,0},{1,25},{9,17},{17,9},{25,1},{2,26},{10... | collective-permute-start | bytes 1179656 | tf_op jit(solution)/shard_map/ppermute | solution.py:309
  33.3 0.5 collective-permute-start.10
  33.8 0.0 collective-permute-done.6
  33.8 0.0 collective-permute-done.refs_0_
  33.8 0.1 add_convert_fusion
  33.9 1.6 %collective-permute-start.9 = (bf16[128,1536]{1,0:T(8,128)(2,1)S(1)}, bf16[128,1536]{1,0:T(8,128)(2,1)S(1)}, u32[]{:S(2)}, u32[]{:S(2)}) collective-permute-start(bf16[128,1536]{1,0:T(8,128)(2,1)S(1)} %add_convert_fusion), channel_id=1, source_target_pairs={{0,2},{1,3},{2,0},{3,1},{4,6},{5,7},{6,4},{7,5},{8,10},{9,11},{10,... | collective-permute-start | bytes 1179656 | tf_op jit(solution)/shard_map/ppermute | solution.py:312
  35.6 0.5 collective-permute-start.8
  36.1 0.1 convert_add_fusion
  36.2 8.3 %collective-permute-done.9 = bf16[128,1536]{1,0:T(8,128)(2,1)S(1)} collective-permute-done((bf16[128,1536]{1,0:T(8,128)(2,1)S(1)}, bf16[128,1536]{1,0:T(8,128)(2,1)S(1)}, u32[]{:S(2)}, u32[]{:S(2)}) %collective-permute-start.9) | collective-permute-done | bytes 393248 | tf_op jit(solution)/shard_map/ppermute | solution.py:312
  44.5 0.1 fusion
  44.6 2.7 %collective-permute-start.12 = (bf16[64,1536]{1,0:T(8,128)(2,1)S(1)}, bf16[64,1536]{1,0:T(8,128)(2,1)S(1)}, u32[]{:S(2)}, u32[]{:S(2)}) collective-permute-start(bf16[64,1536]{1,0:T(8,128)(2,1)S(1)} %get-tuple-element.47), channel_id=1, source_target_pairs={{0,4},{1,5},{2,6},{3,7},{4,0},{5,1},{6,2},{7,3},{8,12},{9,13},{10,... | collective-permute-start | bytes 589832 | tf_op jit(solution)/shard_map/ppermute | solution.py:312
  47.3 0.0 collective-permute-done.8.refs_1_
  47.3 5.6 %weight_gradient.2.refs_3_ = bf16[6144,768]{1,0:T(8,128)(2,1)} custom-call(s32[3]{0:T(128)S(1)} %pad_add_fusion.idx_ref, bf16[128,24576]{1,0:T(8,128)(2,1)} %hidden_hbm.3, bf16[128,1536]{1,0:T(8,128)(2,1)S(1)} %collective-permute-done.1.diag_ref, bf16[128,1536]{1,0:T(8,128)(2,1)S(1)} %collective-permute-done.7.swapped_ref, ...), custom_call_target="tpu_custom_call" | custom-call | flops 1 | bytes 1 | tf_op jit(solution)/shard_map/weight_gradient/pallas_call | solution.py:248
  52.9 0.0 collective-permute-done.10.refs_0_
  52.9 0.1 collective-permute-start.13
  53.0 0.5 collective-permute-start.14
  53.5 1.7 %collective-permute-done.12.refs_1_ = bf16[64,1536]{1,0:T(8,128)(2,1)S(1)} collective-permute-done((bf16[64,1536]{1,0:T(8,128)(2,1)S(1)}, bf16[64,1536]{1,0:T(8,128)(2,1)S(1)}, u32[]{:S(2)}, u32[]{:S(2)}) %collective-permute-start.12) | collective-permute-done | bytes 196640 | tf_op jit(solution)/shard_map/ppermute | solution.py:312
  55.2 1.5 %grad_input.1 = bf16[64,6144]{1,0:T(8,128)(2,1)} custom-call(f32[64,1536]{1,0:T(8,128)S(1)} %get-tuple-element.38.refs_0_, bf16[64,1536]{1,0:T(8,128)(2,1)S(1)} %collective-permute-done.12.refs_1_, bf16[512,128]{1,0:T(8,128)(2,1)S(1)} %copy-done), custom_call_target="tpu_custom_call" | custom-call | flops 68719476736 | bytes 268435456 | tf_op jit(solution)/shard_map/grad_input/pallas_call | solution.py:289
  56.7 0.0 collective-permute-done.13.swapped_ref
  56.7 0.0 collective-permute-done.14.refs_1_
  56.7 5.6 %weight_gradient.3 = bf16[6144,768]{1,0:T(8,128)(2,1)} custom-call(s32[3]{0:T(128)S(1)} %pad_add_fusion.idx_ref, bf16[128,24576]{1,0:T(8,128)(2,1)} %hidden_hbm.3, bf16[128,1536]{1,0:T(8,128)(2,1)S(1)} %collective-permute-done.11.diag_ref, bf16[128,1536]{1,0:T(8,128)(2,1)S(1)} %collective-permute-done.13.swapped_ref, ...), custom_call_target="tpu_custom_call", output_to_operand_aliasing={{}: (7, {})} | custom-call | flops 1 | bytes 1 | tf_op jit(solution)/shard_map/weight_gradient/pallas_call | solution.py:248
  (13 shorter events, 0.0 us)
Async XLA Ops:
  0.6 11.2 %collective-permute-start.3 = (bf16[128,768]{1,0:T(8,128)(2,1)}, bf16[128,768]{1,0:T(8,128)(2,1)S(1)}, u32[]{:S(2)}, u32[]{:S(2)}) collective-permute-start(bf16[128,768]{1,0:T(8,128)(2,1)} %refs_0_.1), channel_id=1, source_target_pairs={{0,16},{8,24},{16,0},{24,8},{1,17},{9,25},{17,1},{25,9},{2,18},{10... | collective-permute-start | bytes 589832 | tf_op jit(solution)/shard_map/ppermute | solution.py:309
  3.7 8.1 %collective-permute-start.2 = (bf16[128,768]{1,0:T(8,128)(2,1)}, bf16[128,768]{1,0:T(8,128)(2,1)S(1)}, u32[]{:S(2)}, u32[]{:S(2)}) collective-permute-start(bf16[128,768]{1,0:T(8,128)(2,1)} %refs_0_.1), channel_id=1, source_target_pairs={{0,8},{8,0},{16,24},{24,16},{1,9},{9,1},{17,25},{25,17},{2,10},{10... | collective-permute-start | bytes 589832 | tf_op jit(solution)/shard_map/ppermute | solution.py:309
  5.2 10.3 %collective-permute-start.4 = (bf16[128,768]{1,0:T(8,128)(2,1)}, bf16[128,768]{1,0:T(8,128)(2,1)S(1)}, u32[]{:S(2)}, u32[]{:S(2)}) collective-permute-start(bf16[128,768]{1,0:T(8,128)(2,1)} %refs_0_.1), channel_id=1, source_target_pairs={{0,24},{8,16},{16,8},{24,0},{1,25},{9,17},{17,9},{25,1},{2,26},{10... | collective-permute-start | bytes 589832 | tf_op jit(solution)/shard_map/ppermute | solution.py:309
  8.3 25.0 %collective-permute-start.1 = (bf16[128,1536]{1,0:T(8,128)(2,1)}, bf16[128,1536]{1,0:T(8,128)(2,1)S(1)}, u32[]{:S(2)}, u32[]{:S(2)}) collective-permute-start(bf16[128,1536]{1,0:T(8,128)(2,1)} %get-tuple-element.26), channel_id=1, source_target_pairs={{0,24},{8,16},{16,8},{24,0},{1,25},{9,17},{17,9},{25,1},{2,26},{10... | collective-permute-start | bytes 1179656 | tf_op jit(solution)/shard_map/ppermute | solution.py:309
  11.3 19.1 %copy-start.2 = (bf16[128,1536]{1,0:T(8,128)(2,1)S(1)}, bf16[128,1536]{1,0:T(8,128)(2,1)}, u32[]{:S(2)}) copy-start(bf16[128,1536]{1,0:T(8,128)(2,1)} %get-tuple-element.37) | copy-start | bytes 1179652
  11.3 22.0 %copy-start.1 = (bf16[128,3072]{1,0:T(8,128)(2,1)S(1)}, bf16[128,3072]{1,0:T(8,128)(2,1)}, u32[]{:S(2)}) copy-start(bf16[128,3072]{1,0:T(8,128)(2,1)} %get-tuple-element.36) | copy-start | bytes 2359300
  11.3 22.6 %collective-permute-start = (bf16[128,3072]{1,0:T(8,128)(2,1)}, bf16[128,3072]{1,0:T(8,128)(2,1)S(1)}, u32[]{:S(2)}, u32[]{:S(2)}) collective-permute-start(bf16[128,3072]{1,0:T(8,128)(2,1)} %get-tuple-element.25), channel_id=1, source_target_pairs={{0,8},{1,17},{2,10},{3,19},{4,12},{5,21},{6,14},{7,23},{8,0},{9,25... | collective-permute-start | bytes 2359304 | tf_op jit(solution)/shard_map/ppermute | solution.py:334
  29.8 4.0 %collective-permute-start.5 = (bf16[128,1536]{1,0:T(8,128)(2,1)S(1)}, bf16[128,1536]{1,0:T(8,128)(2,1)S(1)}, u32[]{:S(2)}, u32[]{:S(2)}) collective-permute-start(bf16[128,1536]{1,0:T(8,128)(2,1)S(1)} %get-tuple-element.27), channel_id=1, source_target_pairs={{0,1},{1,0},{2,3},{3,2},{4,5},{5,4},{6,7},{7,6},{8,9},{9,8},{10,11... | collective-permute-start | bytes 1179656 | tf_op jit(solution)/shard_map/ppermute | solution.py:312
  29.9 4.0 %collective-permute-start.6 = (bf16[128,1536]{1,0:T(8,128)(2,1)S(1)}, bf16[128,1536]{1,0:T(8,128)(2,1)S(1)}, u32[]{:S(2)}, u32[]{:S(2)}) collective-permute-start(bf16[128,1536]{1,0:T(8,128)(2,1)S(1)} %get-tuple-element.28), channel_id=1, source_target_pairs={{0,1},{1,0},{2,3},{3,2},{4,5},{5,4},{6,7},{7,6},{8,9},{9,8},{10,11... | collective-permute-start | bytes 1179656 | tf_op jit(solution)/shard_map/ppermute | solution.py:312
  30.4 22.5 %collective-permute-start.11 = (bf16[128,1536]{1,0:T(8,128)(2,1)S(1)}, bf16[128,1536]{1,0:T(8,128)(2,1)S(1)}, u32[]{:S(2)}, u32[]{:S(2)}) collective-permute-start(bf16[128,1536]{1,0:T(8,128)(2,1)S(1)} %copy-done.2), channel_id=1, source_target_pairs={{0,24},{8,16},{16,8},{24,0},{1,25},{9,17},{17,9},{25,1},{2,26},{10... | collective-permute-start | bytes 1179656 | tf_op jit(solution)/shard_map/ppermute | solution.py:309
  33.3 19.6 %collective-permute-start.10 = (bf16[128,3072]{1,0:T(8,128)(2,1)S(1)}, bf16[128,3072]{1,0:T(8,128)(2,1)S(1)}, u32[]{:S(2)}, u32[]{:S(2)}) collective-permute-start(bf16[128,3072]{1,0:T(8,128)(2,1)S(1)} %copy-done.1), channel_id=1, source_target_pairs={{0,8},{1,17},{2,10},{3,19},{4,12},{5,21},{6,14},{7,23},{8,0},{9,25... | collective-permute-start | bytes 2359304 | tf_op jit(solution)/shard_map/ppermute | solution.py:334
  33.9 10.6 %collective-permute-start.9 = (bf16[128,1536]{1,0:T(8,128)(2,1)S(1)}, bf16[128,1536]{1,0:T(8,128)(2,1)S(1)}, u32[]{:S(2)}, u32[]{:S(2)}) collective-permute-start(bf16[128,1536]{1,0:T(8,128)(2,1)S(1)} %add_convert_fusion), channel_id=1, source_target_pairs={{0,2},{1,3},{2,0},{3,1},{4,6},{5,7},{6,4},{7,5},{8,10},{9,11},{10,... | collective-permute-start | bytes 1179656 | tf_op jit(solution)/shard_map/ppermute | solution.py:312
  35.6 11.7 %collective-permute-start.7 = (bf16[128,1536]{1,0:T(8,128)(2,1)S(1)}, bf16[128,1536]{1,0:T(8,128)(2,1)S(1)}, u32[]{:S(2)}, u32[]{:S(2)}) collective-permute-start(bf16[128,1536]{1,0:T(8,128)(2,1)S(1)} %collective-permute-done.1.diag_ref), channel_id=1, source_target_pairs={{0,1},{1,0},{2,3},{3,2},{4,5},{5,4},{6,7},{7,6},{8,9},{9,8},{10,11... | collective-permute-start | bytes 1179656 | tf_op jit(solution)/shard_map/ppermute | solution.py:312
  35.6 11.7 %collective-permute-start.8 = (bf16[128,3072]{1,0:T(8,128)(2,1)S(1)}, bf16[128,3072]{1,0:T(8,128)(2,1)S(1)}, u32[]{:S(2)}, u32[]{:S(2)}) collective-permute-start(bf16[128,3072]{1,0:T(8,128)(2,1)S(1)} %collective-permute-done.refs_0_), channel_id=1, source_target_pairs={{0,1},{1,0},{2,3},{3,2},{4,5},{5,4},{6,7},{7,6},{8,9},{9,8},{10,11... | collective-permute-start | bytes 2359304 | tf_op jit(solution)/shard_map/ppermute | solution.py:312
  44.6 10.5 %collective-permute-start.12 = (bf16[64,1536]{1,0:T(8,128)(2,1)S(1)}, bf16[64,1536]{1,0:T(8,128)(2,1)S(1)}, u32[]{:S(2)}, u32[]{:S(2)}) collective-permute-start(bf16[64,1536]{1,0:T(8,128)(2,1)S(1)} %get-tuple-element.47), channel_id=1, source_target_pairs={{0,4},{1,5},{2,6},{3,7},{4,0},{5,1},{6,2},{7,3},{8,12},{9,13},{10,... | collective-permute-start | bytes 589832 | tf_op jit(solution)/shard_map/ppermute | solution.py:312
  47.3 7.9 %copy-start = (bf16[512,128]{1,0:T(8,128)(2,1)S(1)}, bf16[512,128]{1,0:T(8,128)(2,1)}, u32[]{:S(2)}) copy-start(bf16[512,128]{1,0:T(8,128)(2,1)} %refs_2_.1) | copy-start | bytes 393220
  52.9 3.8 %collective-permute-start.13 = (bf16[128,1536]{1,0:T(8,128)(2,1)S(1)}, bf16[128,1536]{1,0:T(8,128)(2,1)S(1)}, u32[]{:S(2)}, u32[]{:S(2)}) collective-permute-start(bf16[128,1536]{1,0:T(8,128)(2,1)S(1)} %collective-permute-done.11.diag_ref), channel_id=1, source_target_pairs={{0,1},{1,0},{2,3},{3,2},{4,5},{5,4},{6,7},{7,6},{8,9},{9,8},{10,11... | collective-permute-start | bytes 1179656 | tf_op jit(solution)/shard_map/ppermute | solution.py:312
  53.0 3.7 %collective-permute-start.14 = (bf16[128,3072]{1,0:T(8,128)(2,1)S(1)}, bf16[128,3072]{1,0:T(8,128)(2,1)S(1)}, u32[]{:S(2)}, u32[]{:S(2)}) collective-permute-start(bf16[128,3072]{1,0:T(8,128)(2,1)S(1)} %collective-permute-done.10.refs_0_), channel_id=1, source_target_pairs={{0,1},{1,0},{2,3},{3,2},{4,5},{5,4},{6,7},{7,6},{8,9},{9,8},{10,11... | collective-permute-start | bytes 2359304 | tf_op jit(solution)/shard_map/ppermute | solution.py:312

commit v4 on v3

--- a/solution.py
+++ b/solution.py
@@ -10,7 +10,7 @@
 F32 = jnp.float32
 BF16 = jnp.bfloat16
 MIB = 1024 * 1024
-GW_BLOCKS = 12
+GW_BLOCKS = 8
 LONG = pl.CostEstimate(flops=1 << 36, bytes_accessed=1 << 28, transcendentals=0)
 COST = pl.CostEstimate(flops=1, bytes_accessed=1, transcendentals=0)
 
@@ -59,33 +59,28 @@
         for k in range(nrow):
             grads[rows_at(row ^ k), :] = pieces[k][...]
 
-    tokens = grads.shape[0]
-
-    def product(b, part):
-        cols = slice(part * blk // 2, (part + 1) * blk // 2)
-        units = slice(b * blk + cols.start, b * blk + cols.stop)
+    def product(b):
+        cols = slice(b * blk, (b + 1) * blk)
         partial = lax.dot_general(
-            grads[...], weight_ref[units, :], (((1,), (1,)), ((), ())), preferred_element_type=F32
+            grads[...], weight_ref[cols, :], (((1,), (1,)), ((), ())), preferred_element_type=F32
         )
-        acc_buf[b, :, cols] = partial + feedback_ref[0, :, units].astype(F32)
-
-    def finish(b, part):
-        rows = slice(part * tokens // 2, (part + 1) * tokens // 2)
-        acc = acc_buf[b, rows]
+        acc_buf[b] = partial + feedback_ref[0, :, cols].astype(F32)
+
+    def finish(b):
+        acc = acc_buf[b]
         code = jnp.dot(acc.astype(BF16), compress_ref[...], preferred_element_type=F32)
         code_low = code.astype(BF16)
-        code_buf[rows, b * sub : (b + 1) * sub] = code_low
+        code_buf[:, b * sub : (b + 1) * sub] = code_low
         recon = lax.dot_general(
             code_low, compress_ref[...], (((1,), (1,)), ((), ())), preferred_element_type=F32
         )
-        fresh_ref[0, rows, b * blk : (b + 1) * blk] = (acc - recon).astype(BF16)
-
-    for b in range(count + 1):
-        for part in range(2):
-            if b < count:
-                product(b, part)
-            if b:
-                finish(b - 1, part)
+        fresh_ref[0, :, b * blk : (b + 1) * blk] = (acc - recon).astype(BF16)
+
+    for b in range(count):
+        product(b)
+        if b:
+            finish(b - 1)
+    finish(count - 1)
 
     mine_tokens = grads.shape[0] // ncol
     width = count * sub
@@ -112,7 +107,7 @@
     tokens = feedback.shape[1]
     nblocks = units // blk
     quarter = tokens // 4
-    per = 3 if nblocks % 3 == 0 else 1
+    per = next(n for n in (4, 3, 2, 1) if nblocks % n == 0)
     return pl.pallas_call(
         functools.partial(compress_kernel, nrow, ncol),
         grid_spec=pltpu.PrefetchScalarGridSpec(
@@ -192,80 +187,118 @@
     )(idx, *in_hbm(hidden))
 
 
-def gw_kernel(npieces, low, block, idx_ref, hidden_hbm, diag_ref, swapped_ref, *refs):
-    pieces = refs[:npieces]
-    grads_hbm = refs[npieces]
-    out_hbm, own, grads, out, in_sems, out_sems = refs[-6:]
-    length = own.shape[1]
-    units = out_hbm.shape[0]
-    steps = length // 2 // block
-    row, core = idx_ref[0], idx_ref[1]
+def gw_blocks(core, low, block, own, diag, swapped, pieces, grads, out, out_hbm, sems):
+    steps = diag.shape[1] // block
 
     def columns(i):
         half = core if i < steps else 1 - core
         return pl.ds(pl.multiple_of((half * steps + i % steps) * block, block), block)
 
-    source = pl.ds(pl.multiple_of(row * units + low, block), length)
-    arriving = [
-        pltpu.make_async_copy(hidden_hbm.at[:, source], own, in_sems.at[0]),
-        pltpu.make_async_copy(grads_hbm, grads, in_sems.at[1]),
-    ]
-    for copy in arriving:
-        copy.start()
-    for copy in arriving:
-        copy.wait()
     leaving = []
     for i in range(2 * steps):
-        from_last = diag_ref if i < steps else swapped_ref
+        from_last = diag if i < steps else swapped
         at = (i % steps) * block
         lhs = [own[:, columns(i)], from_last[:, at : at + block]]
         lhs = jnp.concatenate(lhs + [x[:, columns(i)] for x in pieces], axis=0)
         out[i] = lax.dot_general(
             lhs, grads[...], (((0,), (0,)), ((), ())), preferred_element_type=F32
         ).astype(BF16)
-        to = columns(i)
-        to = pl.ds(pl.multiple_of(low + to.start, block), block)
-        leaving.append(pltpu.make_async_copy(out.at[i], out_hbm.at[to, :], out_sems.at[i]))
+        to = pl.ds(pl.multiple_of(low + columns(i).start, block), block)
+        leaving.append(pltpu.make_async_copy(out.at[i], out_hbm.at[to, :], sems.at[i]))
         leaving[-1].start()
     for copy in leaving:
         copy.wait()
 
 
-def gw_call(idx, hidden, diag, swapped, pieces, grads, prev, low, units):
-    tokens, width = grads.shape
-    step_tokens, half = diag.shape
-    block = units // GW_BLOCKS
-    count = 2 * half // block
-    in_specs = [pl.BlockSpec(memory_space=pl.ANY)]
-    in_specs += [pl.BlockSpec(memory_space=pltpu.VMEM)] * (2 + len(pieces))
-    in_specs += [pl.BlockSpec(memory_space=pl.ANY)]
-    args = [*in_hbm(hidden), diag, swapped, *pieces, *in_hbm(grads)]
-    aliases = {}
-    if prev is not None:
-        in_specs += [pl.BlockSpec(memory_space=pl.ANY)]
-        args += [prev]
-        aliases = {len(args): 0}
+def gw_first_kernel(npieces, lows, block, idx_ref, hidden_hbm, diag, swapped, *refs):
+    pieces = refs[:npieces]
+    grads_hbm, out_hbm, own_next, grads, own, out, in_sems, out_sems = refs[npieces:]
+    units = out_hbm.shape[0]
+    row, core = idx_ref[0], idx_ref[1]
+
+    def arriving(i, to):
+        source = pl.ds(pl.multiple_of(row * units + lows[i], block), to.shape[1])
+        return pltpu.make_async_copy(hidden_hbm.at[:, source], to, in_sems.at[i])
+
+    copies = [
+        arriving(0, own),
+        pltpu.make_async_copy(grads_hbm, grads, in_sems.at[2]),
+        arriving(1, own_next),
+    ]
+    for copy in copies:
+        copy.start()
+    for copy in copies:
+        copy.wait()
+    gw_blocks(core, lows[0], block, own, diag, swapped, pieces, grads, out, out_hbm, out_sems)
+
+
+def gw_last_kernel(npieces, low, block, idx_ref, own, diag, swapped, *refs):
+    pieces = refs[:npieces]
+    grads, _, out_hbm, out, sems = refs[npieces:]
+    gw_blocks(idx_ref[1], low, block, own, diag, swapped, pieces, grads, out, out_hbm, sems)
+
+
+def gw_call(kernel, idx, args, spaces, count, block, outs, scratch, aliases):
+    width = outs[0].shape[1]
     return pl.pallas_call(
-        functools.partial(gw_kernel, len(pieces), low, block),
+        kernel,
         grid_spec=pltpu.PrefetchScalarGridSpec(
             num_scalar_prefetch=1,
             grid=(1,),
-            in_specs=in_specs,
-            out_specs=pl.BlockSpec(memory_space=pl.ANY),
+            in_specs=[pl.BlockSpec(memory_space=space) for space in spaces],
+            out_specs=[pl.BlockSpec(memory_space=pl.ANY)]
+            + [pl.BlockSpec(memory_space=pltpu.VMEM)] * (len(outs) - 1),
             scratch_shapes=[
-                pltpu.VMEM((step_tokens, 2 * half), BF16),
-                pltpu.VMEM((tokens, width), BF16),
+                *scratch,
                 pltpu.VMEM((count, block, width), BF16),
-                pltpu.SemaphoreType.DMA((2,)),
+                *([pltpu.SemaphoreType.DMA((3,))] if scratch else []),
                 pltpu.SemaphoreType.DMA((count,)),
             ],
         ),
-        out_shape=pltpu.HBM((units, width), BF16),
+        out_shape=outs,
         input_output_aliases=aliases,
         compiler_params=pltpu.CompilerParams(vmem_limit_bytes=28 * MIB),
         cost_estimate=COST,
         name="weight_gradient",
     )(idx, *args)
+
+
+def gw_first(idx, hidden, diag, swapped, pieces, grads, lows, units):
+    tokens, width = grads.shape
+    step_tokens, half = diag.shape
+    block = units // GW_BLOCKS
+    return gw_call(
+        functools.partial(gw_first_kernel, len(pieces), lows, block),
+        idx,
+        [*in_hbm(hidden), diag, swapped, *pieces, *in_hbm(grads)],
+        [pl.ANY] + [pltpu.VMEM] * (2 + len(pieces)) + [pl.ANY],
+        2 * half // block,
+        block,
+        [
+            pltpu.HBM((units, width), BF16),
+            jax.ShapeDtypeStruct((step_tokens, units - lows[1]), BF16),
+            jax.ShapeDtypeStruct((tokens, width), BF16),
+        ],
+        [pltpu.VMEM((step_tokens, 2 * half), BF16)],
+        {},
+    )
+
+
+def gw_last(idx, own, diag, swapped, pieces, grads, prev, low):
+    block = prev.shape[0] // GW_BLOCKS
+    args = [own, diag, swapped, *pieces, grads, prev]
+    (grad_weight,) = gw_call(
+        functools.partial(gw_last_kernel, len(pieces), low, block),
+        idx,
+        args,
+        [pltpu.VMEM] * (len(args) - 1) + [pl.ANY],
+        2 * diag.shape[1] // block,
+        block,
+        [pltpu.HBM(prev.shape, BF16)],
+        [],
+        {len(args): 0},
+    )
+    return grad_weight
 
 
 def gi_kernel(parts, *refs):
@@ -320,7 +353,7 @@
         ]
 
     pairs = range(1, nrow - 1, 2)
-    lows, lengths = [0, units // 2], [units // 2] * 2
+    lows, lengths = [0, units // 4 * 3], [units // 4 * 3, units // 4]
     firsts, sizes = [], []
     for low, length in zip(lows, lengths):
         firsts += [lambda r, e, k=k, low=low: (r ^ (k + e)) * units + low for k in pairs]
@@ -340,11 +373,14 @@
 
     early = fetch(packed[: len(pairs) + 1])
     new_feedback, *codes, ordered = compress_call(idx, grads, weight, feedback, compress, ncol)
-    late = fetch(packed[len(pairs) + 1 :])
-
-    *others, kept, send = after((*early, *[over_col(x, 1) for x in codes[2:]]))
-    early = list(swap(others))
+
+    early[-1], kept, send = after((early[-1], *[over_col(x, 1) for x in codes[2:]]))
+    *direct, packed = packed[len(pairs) + 1 :]
+    packed, early[0] = after((packed, early[0]))
+    early = swap(early)
     kept, send = [x.astype(F32) + y.astype(F32) for x, y in zip(codes[:2], (kept, send))]
+    send, *direct = after((send.astype(BF16), *direct))
+    late = fetch([*direct, packed])
     step = 1
     while True:
         received = over_col(send.astype(BF16), 2 * step)
@@ -355,12 +391,12 @@
         send = kept[size:] + received[size:].astype(F32)
         kept = kept[:size] + received[:size].astype(F32)
 
-    grad_weight = gw_call(idx, hidden, *early, ordered, None, lows[0], units)
+    grad_weight, own, grads = gw_first(idx, hidden, *early, ordered, lows, units)
     grad_weight, kept, *late = after((grad_weight, kept, *late))
     grad_input = gi_call([kept], [received], compress, units)
     diag, swapped, pieces = swap(late)
     grad_input, swapped, *pieces = after((grad_input, swapped, *pieces))
-    grad_weight = gw_call(idx, hidden, diag, swapped, pieces, ordered, grad_weight, lows[1], units)
+    grad_weight = gw_last(idx, own, diag, swapped, pieces, grads, grad_weight, lows[1])
     return (grad_input, grad_weight, new_feedback)
 
 

time: 62.5 us -> 60.1 us (0.962)
  waiting for transfers between devices: 13.7 us -> 12 us
  Pallas kernels: 30.1 us -> 29.2 us
    ppermute x8, waiting for transfers between devices: 10 us -> 4.38 us  [over_col(): return lax.ppermute(x, 'col', xor_perm(ncol, k))]
    ppermute x2, waiting for transfers between devices: 0.01 us -> 4.03 us  [fetch(): lax.ppermute(x, ('row', 'col'), joint_perm(k))]
    ppermute x2, starting transfers between devices: 1.07 us -> 2.02 us  [fetch(): lax.ppermute(x, ('row', 'col'), joint_perm(k))]
    pallas_call x2, Pallas kernels: 11.2 us -> 10.3 us  [gw_call(): pl.pallas_call(kernel, grid_spec=pltpu.PrefetchScalarGridSpec(num_scalar_...]
    ppermute x5, starting transfers between devices: 10.4 us -> 9.64 us  [over_row(): return lax.ppermute(x, 'row', xor_perm(nrow, k))]
  transfers between devices with their start and end apart: 15 -> 15, of which waited for: 3 -> 6; matrix products, arithmetic and copies ran while one was open for 1% -> 1% of each run, Pallas kernels for 39% -> 44%
where the time goes in v4:
time: 60.1 us; the launch traced here: 59.9 us
  Pallas kernels  29.2 us (49%)
  starting transfers between devices  17.7 us (29%)
  waiting for transfers between devices  12 us (20%)
  between operations  0.73 us (1%)
    pallas_call x1, Pallas kernels, compress_call(): pl.pallas_call(functools.partial(compress_kernel, nrow, ncol), grid_spec=...  14.2 us
    pallas_call x2, Pallas kernels, gw_call(): pl.pallas_call(kernel, grid_spec=pltpu.PrefetchScalarGridSpec(num_scalar_...  10.3 us
    ppermute x5, starting transfers between devices, over_row(): return lax.ppermute(x, 'row', xor_perm(nrow, k))  9.64 us
    ppermute x8, starting transfers between devices, over_col(): return lax.ppermute(x, 'col', xor_perm(ncol, k))  6.06 us
    ppermute x8, waiting for transfers between devices, over_col(): return lax.ppermute(x, 'col', xor_perm(ncol, k))  4.38 us
    ppermute x2, waiting for transfers between devices, fetch(): lax.ppermute(x, ('row', 'col'), joint_perm(k))  4.03 us
    ppermute x5, waiting for transfers between devices, over_row(): return lax.ppermute(x, 'row', xor_perm(nrow, k))  3.54 us
    pallas_call x1, Pallas kernels, pack_call(): pl.pallas_call(functools.partial(pack_kernel, parts), grid_spec=pltpu.Pre...  3.18 us
  transfers between devices with their start and end apart: 15, of which 6 were waited for; matrix products, arithmetic and copies ran while one was open for 1% of the time, Pallas kernels for 44%

profile of v4, /device:TPU:0, one launch (start us, length us, event | category | flops | bytes accessed | tf_op | source)
XLA Modules:
  0.0 59.9 jit_solution(4840795965038536903)
XLA Ops:
  0.6 3.0 %collective-permute-start.2 = (bf16[128,768]{1,0:T(8,128)(2,1)}, bf16[128,768]{1,0:T(8,128)(2,1)S(1)}, u32[]{:S(2)}, u32[]{:S(2)}) collective-permute-start(bf16[128,768]{1,0:T(8,128)(2,1)} %refs_0_.1), channel_id=1, source_target_pairs={{0,16},{8,24},{16,0},{24,8},{1,17},{9,25},{17,1},{25,9},{2,18},{10... | collective-permute-start | bytes 589832 | tf_op jit(solution)/shard_map/ppermute | solution.py:342
  3.7 1.5 %collective-permute-start.1 = (bf16[128,768]{1,0:T(8,128)(2,1)}, bf16[128,768]{1,0:T(8,128)(2,1)S(1)}, u32[]{:S(2)}, u32[]{:S(2)}) collective-permute-start(bf16[128,768]{1,0:T(8,128)(2,1)} %refs_0_.1), channel_id=1, source_target_pairs={{0,8},{8,0},{16,24},{24,16},{1,9},{9,1},{17,25},{25,17},{2,10},{10... | collective-permute-start | bytes 589832 | tf_op jit(solution)/shard_map/ppermute | solution.py:342
  5.2 0.1 collective-permute-start.3
  5.2 0.1 pad_add_fusion.idx_ref
  5.3 3.2 %pack_hidden.1 = (bf16[128,4608]{1,0:T(8,128)(2,1)}, bf16[128,2304]{1,0:T(8,128)(2,1)}, bf16[128,1536]{1,0:T(8,128)(2,1)}, bf16[128,768]{1,0:T(8,128)(2,1)}) custom-call(s32[3]{0:T(128)S(1)} %pad_add_fusion.idx_ref, bf16[128,24576]{1,0:T(8,128)(2,1)} %hidden_hbm.1), custom_call_target="tpu_custom_call" | custom-call | flops 1 | bytes 1 | tf_op jit(solution)/shard_map/pack_hidden/pallas_call | solution.py:171
  8.5 2.9 %collective-permute-start = (bf16[128,2304]{1,0:T(8,128)(2,1)}, bf16[128,2304]{1,0:T(8,128)(2,1)S(1)}, u32[]{:S(2)}, u32[]{:S(2)}) collective-permute-start(bf16[128,2304]{1,0:T(8,128)(2,1)} %get-tuple-element.31), channel_id=1, source_target_pairs={{0,24},{8,16},{16,8},{24,0},{1,25},{9,17},{17,9},{25,1},{2,26},{10... | collective-permute-start | bytes 1769480 | tf_op jit(solution)/shard_map/ppermute | solution.py:342
  11.4 0.5 collective-permute-start.7
  11.9 0.0 collective-permute-done.2.refs_2_
  12.0 0.0 collective-permute-done.1.refs_1_
  12.0 3.5 %collective-permute-done.3.refs_3_ = bf16[128,768]{1,0:T(8,128)(2,1)S(1)} collective-permute-done((bf16[128,768]{1,0:T(8,128)(2,1)}, bf16[128,768]{1,0:T(8,128)(2,1)S(1)}, u32[]{:S(2)}, u32[]{:S(2)}) %collective-permute-start.3) | collective-permute-done | bytes 196640 | tf_op jit(solution)/shard_map/ppermute | solution.py:342
  15.5 14.2 %compress_codes.1 = (bf16[1,512,6144]{2,1,0:T(8,128)(2,1)}, bf16[128,1536]{1,0:T(8,128)(2,1)S(1)}, bf16[128,1536]{1,0:T(8,128)(2,1)S(1)}, bf16[128,1536]{1,0:T(8...) custom-call(s32[3]{0:T(128)S(1)} %pad_add_fusion.idx_ref, bf16[128,768]{1,0:T(8,128)(2,1)} %refs_0_.1, ...), custom_call_target="tpu_custom_call" | custom-call | flops 68719476736 | bytes 268435456 | tf_op jit(solution)/shard_map/compress_codes/pallas_call | solution.py:111
  29.7 0.1 collective-permute-start.4
  29.8 0.5 collective-permute-start.5
  30.3 0.0 collective-permute-done.diag
  30.3 1.2 %collective-permute-done.4 = bf16[128,1536]{1,0:T(8,128)(2,1)S(1)} collective-permute-done((bf16[128,1536]{1,0:T(8,128)(2,1)S(1)}, bf16[128,1536]{1,0:T(8,128)(2,1)S(1)}, u32[]{:S(2)}, u32[]{:S(2)}) %collective-permute-start.4) | collective-permute-done | bytes 393248 | tf_op jit(solution)/shard_map/ppermute | solution.py:345
  31.5 0.6 collective-permute-done.5
  32.0 0.1 add_convert_fusion
  32.1 2.1 %collective-permute-start.9 = (bf16[128,1536]{1,0:T(8,128)(2,1)S(1)}, bf16[128,1536]{1,0:T(8,128)(2,1)S(1)}, u32[]{:S(2)}, u32[]{:S(2)}) collective-permute-start(bf16[128,1536]{1,0:T(8,128)(2,1)S(1)} %add_convert_fusion), channel_id=1, source_target_pairs={{0,2},{1,3},{2,0},{3,1},{4,6},{5,7},{6,4},{7,5},{8,10},{9,11},{10,... | collective-permute-start | bytes 1179656 | tf_op jit(solution)/shard_map/ppermute | solution.py:345
  34.3 1.5 %collective-permute-start.10 = (bf16[128,1536]{1,0:T(8,128)(2,1)S(1)}, bf16[128,1536]{1,0:T(8,128)(2,1)S(1)}, u32[]{:S(2)}, u32[]{:S(2)}) collective-permute-start(bf16[128,1536]{1,0:T(8,128)(2,1)S(1)} %copy-done.1), channel_id=1, source_target_pairs={{0,8},{1,17},{2,10},{3,19},{4,12},{5,21},{6,14},{7,23},{8,0},{9,25... | collective-permute-start | bytes 1179656 | tf_op jit(solution)/shard_map/ppermute | solution.py:367
  35.7 4.0 %collective-permute-done.7.refs_0_ = bf16[128,4608]{1,0:T(8,128)(2,1)S(1)} collective-permute-done((bf16[128,4608]{1,0:T(8,128)(2,1)}, bf16[128,4608]{1,0:T(8,128)(2,1)S(1)}, u32[]{:S(2)}, u32[]{:S(2)}) %collective-permute-start.7) | collective-permute-done | bytes 1179680 | tf_op jit(solution)/shard_map/ppermute | solution.py:367
  39.8 0.1 convert_add_fusion
  39.9 0.0 copy-start
  39.9 2.1 %collective-permute-start.11 = (bf16[128,768]{1,0:T(8,128)(2,1)S(1)}, bf16[128,768]{1,0:T(8,128)(2,1)S(1)}, u32[]{:S(2)}, u32[]{:S(2)}) collective-permute-start(bf16[128,768]{1,0:T(8,128)(2,1)S(1)} %copy-done.2), channel_id=1, source_target_pairs={{0,24},{8,16},{16,8},{24,0},{1,25},{9,17},{17,9},{25,1},{2,26},{10... | collective-permute-start | bytes 589832 | tf_op jit(solution)/shard_map/ppermute | solution.py:342
  42.0 1.6 %collective-permute-done.9 = bf16[128,1536]{1,0:T(8,128)(2,1)S(1)} collective-permute-done((bf16[128,1536]{1,0:T(8,128)(2,1)S(1)}, bf16[128,1536]{1,0:T(8,128)(2,1)S(1)}, u32[]{:S(2)}, u32[]{:S(2)}) %collective-permute-start.9) | collective-permute-done | bytes 393248 | tf_op jit(solution)/shard_map/ppermute | solution.py:345
  43.7 0.1 fusion
  43.7 2.8 %collective-permute-start.12 = (bf16[64,1536]{1,0:T(8,128)(2,1)S(1)}, bf16[64,1536]{1,0:T(8,128)(2,1)S(1)}, u32[]{:S(2)}, u32[]{:S(2)}) collective-permute-start(bf16[64,1536]{1,0:T(8,128)(2,1)S(1)} %get-tuple-element.59), channel_id=1, source_target_pairs={{0,4},{1,5},{2,6},{3,7},{4,0},{5,1},{6,2},{7,3},{8,12},{9,13},{10,... | collective-permute-start | bytes 589832 | tf_op jit(solution)/shard_map/ppermute | solution.py:345
  46.6 7.2 %weight_gradient.2 = (bf16[6144,768]{1,0:T(8,128)(2,1)}, bf16[128,1536]{1,0:T(8,128)(2,1)S(1)}, bf16[512,768]{1,0:T(8,128)(2,1)S(1)}) custom-call(s32[3]{0:T(128)S(1)} %pad_add_fusion.idx_ref, bf16[128,24576]{1,0:T(8,128)(2,1)} %hidden_hbm.1, bf16[128,2304]{1,0:T(8,128)(2,1)S(1)} %collective-permute-done.diag, ...), custom_call_target="tpu_custom_call" | custom-call | flops 1 | bytes 1 | tf_op jit(solution)/shard_map/weight_gradient/pallas_call | solution.py:243
  53.8 0.1 collective-permute-start.13
  53.9 0.5 collective-permute-start.14
  54.4 1.0 %collective-permute-done.12.refs_1_ = bf16[64,1536]{1,0:T(8,128)(2,1)S(1)} collective-permute-done((bf16[64,1536]{1,0:T(8,128)(2,1)S(1)}, bf16[64,1536]{1,0:T(8,128)(2,1)S(1)}, u32[]{:S(2)}, u32[]{:S(2)}) %collective-permute-start.12) | collective-permute-done | bytes 196640 | tf_op jit(solution)/shard_map/ppermute | solution.py:345
  55.3 1.5 %grad_input.1 = bf16[64,6144]{1,0:T(8,128)(2,1)} custom-call(f32[64,1536]{1,0:T(8,128)S(1)} %get-tuple-element.48.refs_0_, bf16[64,1536]{1,0:T(8,128)(2,1)S(1)} %collective-permute-done.12.refs_1_, bf16[512,128]{1,0:T(8,128)(2,1)S(1)} %copy-done), custom_call_target="tpu_custom_call" | custom-call | flops 68719476736 | bytes 268435456 | tf_op jit(solution)/shard_map/grad_input/pallas_call | solution.py:322
  56.9 3.0 %weight_gradient.3 = bf16[6144,768]{1,0:T(8,128)(2,1)} custom-call(s32[3]{0:T(128)S(1)} %pad_add_fusion.idx_ref, bf16[128,1536]{1,0:T(8,128)(2,1)S(1)} %get-tuple-element.52.own, bf16[128,768]{1,0:T(8,128)(2,1)S(1)} %collective-permute-done.11.diag, bf16[128,768]{1,0:T(8,128)(2,1)S(1)} %collective-permute-done.13.swapped, ...), custom_call_target="tpu_custom_call", output_to_operand_aliasing={{}: (7, {})} | custom-call | flops 1 | bytes 1 | tf_op jit(solution)/shard_map/weight_gradient/pallas_call | solution.py:243
  (13 shorter events, 0.0 us)
Async XLA Ops:
  0.6 11.3 %collective-permute-start.2 = (bf16[128,768]{1,0:T(8,128)(2,1)}, bf16[128,768]{1,0:T(8,128)(2,1)S(1)}, u32[]{:S(2)}, u32[]{:S(2)}) collective-permute-start(bf16[128,768]{1,0:T(8,128)(2,1)} %refs_0_.1), channel_id=1, source_target_pairs={{0,16},{8,24},{16,0},{24,8},{1,17},{9,25},{17,1},{25,9},{2,18},{10... | collective-permute-start | bytes 589832 | tf_op jit(solution)/shard_map/ppermute | solution.py:342
  3.7 8.3 %collective-permute-start.1 = (bf16[128,768]{1,0:T(8,128)(2,1)}, bf16[128,768]{1,0:T(8,128)(2,1)S(1)}, u32[]{:S(2)}, u32[]{:S(2)}) collective-permute-start(bf16[128,768]{1,0:T(8,128)(2,1)} %refs_0_.1), channel_id=1, source_target_pairs={{0,8},{8,0},{16,24},{24,16},{1,9},{9,1},{17,25},{25,17},{2,10},{10... | collective-permute-start | bytes 589832 | tf_op jit(solution)/shard_map/ppermute | solution.py:342
  5.2 10.3 %collective-permute-start.3 = (bf16[128,768]{1,0:T(8,128)(2,1)}, bf16[128,768]{1,0:T(8,128)(2,1)S(1)}, u32[]{:S(2)}, u32[]{:S(2)}) collective-permute-start(bf16[128,768]{1,0:T(8,128)(2,1)} %refs_0_.1), channel_id=1, source_target_pairs={{0,24},{8,16},{16,8},{24,0},{1,25},{9,17},{17,9},{25,1},{2,26},{10... | collective-permute-start | bytes 589832 | tf_op jit(solution)/shard_map/ppermute | solution.py:342
  8.5 21.8 %collective-permute-start = (bf16[128,2304]{1,0:T(8,128)(2,1)}, bf16[128,2304]{1,0:T(8,128)(2,1)S(1)}, u32[]{:S(2)}, u32[]{:S(2)}) collective-permute-start(bf16[128,2304]{1,0:T(8,128)(2,1)} %get-tuple-element.31), channel_id=1, source_target_pairs={{0,24},{8,16},{16,8},{24,0},{1,25},{9,17},{17,9},{25,1},{2,26},{10... | collective-permute-start | bytes 1769480 | tf_op jit(solution)/shard_map/ppermute | solution.py:342
  11.4 22.8 %copy-start.1 = (bf16[128,1536]{1,0:T(8,128)(2,1)S(1)}, bf16[128,1536]{1,0:T(8,128)(2,1)}, u32[]{:S(2)}) copy-start(bf16[128,1536]{1,0:T(8,128)(2,1)} %get-tuple-element.46) | copy-start | bytes 1179652
  11.4 28.5 %copy-start.2 = (bf16[128,768]{1,0:T(8,128)(2,1)S(1)}, bf16[128,768]{1,0:T(8,128)(2,1)}, u32[]{:S(2)}) copy-start(bf16[128,768]{1,0:T(8,128)(2,1)} %get-tuple-element.47) | copy-start | bytes 589828
  11.4 28.4 %collective-permute-start.7 = (bf16[128,4608]{1,0:T(8,128)(2,1)}, bf16[128,4608]{1,0:T(8,128)(2,1)S(1)}, u32[]{:S(2)}, u32[]{:S(2)}) collective-permute-start(bf16[128,4608]{1,0:T(8,128)(2,1)} %get-tuple-element.36), channel_id=1, source_target_pairs={{0,8},{1,17},{2,10},{3,19},{4,12},{5,21},{6,14},{7,23},{8,0},{9,25... | collective-permute-start | bytes 3538952 | tf_op jit(solution)/shard_map/ppermute | solution.py:367
  29.7 1.8 %collective-permute-start.4 = (bf16[128,1536]{1,0:T(8,128)(2,1)S(1)}, bf16[128,1536]{1,0:T(8,128)(2,1)S(1)}, u32[]{:S(2)}, u32[]{:S(2)}) collective-permute-start(bf16[128,1536]{1,0:T(8,128)(2,1)S(1)} %get-tuple-element.32), channel_id=1, source_target_pairs={{0,1},{1,0},{2,3},{3,2},{4,5},{5,4},{6,7},{7,6},{8,9},{9,8},{10,11... | collective-permute-start | bytes 1179656 | tf_op jit(solution)/shard_map/ppermute | solution.py:345
  29.8 2.3 %collective-permute-start.5 = (bf16[128,1536]{1,0:T(8,128)(2,1)S(1)}, bf16[128,1536]{1,0:T(8,128)(2,1)S(1)}, u32[]{:S(2)}, u32[]{:S(2)}) collective-permute-start(bf16[128,1536]{1,0:T(8,128)(2,1)S(1)} %get-tuple-element.33), channel_id=1, source_target_pairs={{0,1},{1,0},{2,3},{3,2},{4,5},{5,4},{6,7},{7,6},{8,9},{9,8},{10,11... | collective-permute-start | bytes 1179656 | tf_op jit(solution)/shard_map/ppermute | solution.py:345
  32.1 11.5 %collective-permute-start.9 = (bf16[128,1536]{1,0:T(8,128)(2,1)S(1)}, bf16[128,1536]{1,0:T(8,128)(2,1)S(1)}, u32[]{:S(2)}, u32[]{:S(2)}) collective-permute-start(bf16[128,1536]{1,0:T(8,128)(2,1)S(1)} %add_convert_fusion), channel_id=1, source_target_pairs={{0,2},{1,3},{2,0},{3,1},{4,6},{5,7},{6,4},{7,5},{8,10},{9,11},{10,... | collective-permute-start | bytes 1179656 | tf_op jit(solution)/shard_map/ppermute | solution.py:345
  34.3 19.5 %collective-permute-start.10 = (bf16[128,1536]{1,0:T(8,128)(2,1)S(1)}, bf16[128,1536]{1,0:T(8,128)(2,1)S(1)}, u32[]{:S(2)}, u32[]{:S(2)}) collective-permute-start(bf16[128,1536]{1,0:T(8,128)(2,1)S(1)} %copy-done.1), channel_id=1, source_target_pairs={{0,8},{1,17},{2,10},{3,19},{4,12},{5,21},{6,14},{7,23},{8,0},{9,25... | collective-permute-start | bytes 1179656 | tf_op jit(solution)/shard_map/ppermute | solution.py:367
  35.7 10.8 %collective-permute-start.6 = (bf16[128,2304]{1,0:T(8,128)(2,1)S(1)}, bf16[128,2304]{1,0:T(8,128)(2,1)S(1)}, u32[]{:S(2)}, u32[]{:S(2)}) collective-permute-start(bf16[128,2304]{1,0:T(8,128)(2,1)S(1)} %collective-permute-done.diag), channel_id=1, source_target_pairs={{0,1},{1,0},{2,3},{3,2},{4,5},{5,4},{6,7},{7,6},{8,9},{9,8},{10,11... | collective-permute-start | bytes 1769480 | tf_op jit(solution)/shard_map/ppermute | solution.py:345
  39.8 6.8 %collective-permute-start.8 = (bf16[128,4608]{1,0:T(8,128)(2,1)S(1)}, bf16[128,4608]{1,0:T(8,128)(2,1)S(1)}, u32[]{:S(2)}, u32[]{:S(2)}) collective-permute-start(bf16[128,4608]{1,0:T(8,128)(2,1)S(1)} %collective-permute-done.7.refs_0_), channel_id=1, source_target_pairs={{0,1},{1,0},{2,3},{3,2},{4,5},{5,4},{6,7},{7,6},{8,9},{9,8},{10,11... | collective-permute-start | bytes 3538952 | tf_op jit(solution)/shard_map/ppermute | solution.py:345
  39.9 15.5 %copy-start = (bf16[512,128]{1,0:T(8,128)(2,1)S(1)}, bf16[512,128]{1,0:T(8,128)(2,1)}, u32[]{:S(2)}) copy-start(bf16[512,128]{1,0:T(8,128)(2,1)} %refs_2_.1) | copy-start | bytes 393220
  39.9 13.9 %collective-permute-start.11 = (bf16[128,768]{1,0:T(8,128)(2,1)S(1)}, bf16[128,768]{1,0:T(8,128)(2,1)S(1)}, u32[]{:S(2)}, u32[]{:S(2)}) collective-permute-start(bf16[128,768]{1,0:T(8,128)(2,1)S(1)} %copy-done.2), channel_id=1, source_target_pairs={{0,24},{8,16},{16,8},{24,0},{1,25},{9,17},{17,9},{25,1},{2,26},{10... | collective-permute-start | bytes 589832 | tf_op jit(solution)/shard_map/ppermute | solution.py:342
  43.7 11.6 %collective-permute-start.12 = (bf16[64,1536]{1,0:T(8,128)(2,1)S(1)}, bf16[64,1536]{1,0:T(8,128)(2,1)S(1)}, u32[]{:S(2)}, u32[]{:S(2)}) collective-permute-start(bf16[64,1536]{1,0:T(8,128)(2,1)S(1)} %get-tuple-element.59), channel_id=1, source_target_pairs={{0,4},{1,5},{2,6},{3,7},{4,0},{5,1},{6,2},{7,3},{8,12},{9,13},{10,... | collective-permute-start | bytes 589832 | tf_op jit(solution)/shard_map/ppermute | solution.py:345
  53.8 3.1 %collective-permute-start.13 = (bf16[128,768]{1,0:T(8,128)(2,1)S(1)}, bf16[128,768]{1,0:T(8,128)(2,1)S(1)}, u32[]{:S(2)}, u32[]{:S(2)}) collective-permute-start(bf16[128,768]{1,0:T(8,128)(2,1)S(1)} %collective-permute-done.11.diag), channel_id=1, source_target_pairs={{0,1},{1,0},{2,3},{3,2},{4,5},{5,4},{6,7},{7,6},{8,9},{9,8},{10,11... | collective-permute-start | bytes 589832 | tf_op jit(solution)/shard_map/ppermute | solution.py:345
  53.9 3.0 %collective-permute-start.14 = (bf16[128,1536]{1,0:T(8,128)(2,1)S(1)}, bf16[128,1536]{1,0:T(8,128)(2,1)S(1)}, u32[]{:S(2)}, u32[]{:S(2)}) collective-permute-start(bf16[128,1536]{1,0:T(8,128)(2,1)S(1)} %collective-permute-done.10.refs_0_), channel_id=1, source_target_pairs={{0,1},{1,0},{2,3},{3,2},{4,5},{5,4},{6,7},{7,6},{8,9},{9,8},{10,11... | collective-permute-start | bytes 1179656 | tf_op jit(solution)/shard_map/ppermute | solution.py:345

commit v5 on v4

--- a/solution.py
+++ b/solution.py
@@ -374,7 +374,8 @@
     early = fetch(packed[: len(pairs) + 1])
     new_feedback, *codes, ordered = compress_call(idx, grads, weight, feedback, compress, ncol)
 
-    early[-1], kept, send = after((early[-1], *[over_col(x, 1) for x in codes[2:]]))
+    kept, send = [over_col(x, 1) for x in codes[2:]]
+    early[-1], send = after((early[-1], send))
     *direct, packed = packed[len(pairs) + 1 :]
     packed, early[0] = after((packed, early[0]))
     early = swap(early)

time: 60.1 us -> 59.5 us (0.990)
    ppermute x8, waiting for transfers between devices: 4.38 us -> 3.26 us  [over_col(): return lax.ppermute(x, 'col', xor_perm(ncol, k))]
  transfers between devices with their start and end apart: 15 -> 15, of which waited for: 6 -> 5; matrix products, arithmetic and copies ran while one was open for 1% -> 1% of each run, Pallas kernels for 44% -> 44%
where the time goes in v5:
time: 59.5 us; the launch traced here: 59.4 us
  Pallas kernels  29.2 us (49%)
  starting transfers between devices  17.7 us (30%)
  waiting for transfers between devices  11.4 us (19%)
  between operations  0.73 us (1%)
    pallas_call x1, Pallas kernels, compress_call(): pl.pallas_call(functools.partial(compress_kernel, nrow, ncol), grid_spec=...  14.2 us
    pallas_call x2, Pallas kernels, gw_call(): pl.pallas_call(kernel, grid_spec=pltpu.PrefetchScalarGridSpec(num_scalar_...  10.3 us
    ppermute x5, starting transfers between devices, over_row(): return lax.ppermute(x, 'row', xor_perm(nrow, k))  9.64 us
    ppermute x8, starting transfers between devices, over_col(): return lax.ppermute(x, 'col', xor_perm(ncol, k))  6.06 us
    ppermute x2, waiting for transfers between devices, fetch(): lax.ppermute(x, ('row', 'col'), joint_perm(k))  4.59 us
    ppermute x5, waiting for transfers between devices, over_row(): return lax.ppermute(x, 'row', xor_perm(nrow, k))  3.54 us
    ppermute x8, waiting for transfers between devices, over_col(): return lax.ppermute(x, 'col', xor_perm(ncol, k))  3.26 us
    pallas_call x1, Pallas kernels, pack_call(): pl.pallas_call(functools.partial(pack_kernel, parts), grid_spec=pltpu.Pre...  3.18 us
  transfers between devices with their start and end apart: 15, of which 5 were waited for; matrix products, arithmetic and copies ran while one was open for 1% of the time, Pallas kernels for 44%

profile of v5, /device:TPU:0, one launch (start us, length us, event | category | flops | bytes accessed | tf_op | source)
XLA Modules:
  0.0 59.4 jit_solution(8305875318666796303)
XLA Ops:
  0.6 3.0 %collective-permute-start.2 = (bf16[128,768]{1,0:T(8,128)(2,1)}, bf16[128,768]{1,0:T(8,128)(2,1)S(1)}, u32[]{:S(2)}, u32[]{:S(2)}) collective-permute-start(bf16[128,768]{1,0:T(8,128)(2,1)} %refs_0_.1), channel_id=1, source_target_pairs={{0,16},{8,24},{16,0},{24,8},{1,17},{9,25},{17,1},{25,9},{2,18},{10... | collective-permute-start | bytes 589832 | tf_op jit(solution)/shard_map/ppermute | solution.py:342
  3.7 1.5 %collective-permute-start.1 = (bf16[128,768]{1,0:T(8,128)(2,1)}, bf16[128,768]{1,0:T(8,128)(2,1)S(1)}, u32[]{:S(2)}, u32[]{:S(2)}) collective-permute-start(bf16[128,768]{1,0:T(8,128)(2,1)} %refs_0_.1), channel_id=1, source_target_pairs={{0,8},{8,0},{16,24},{24,16},{1,9},{9,1},{17,25},{25,17},{2,10},{10... | collective-permute-start | bytes 589832 | tf_op jit(solution)/shard_map/ppermute | solution.py:342
  5.2 0.1 collective-permute-start.3
  5.2 0.1 pad_add_fusion.idx_ref
  5.3 3.2 %pack_hidden.1 = (bf16[128,4608]{1,0:T(8,128)(2,1)}, bf16[128,2304]{1,0:T(8,128)(2,1)}, bf16[128,1536]{1,0:T(8,128)(2,1)}, bf16[128,768]{1,0:T(8,128)(2,1)}) custom-call(s32[3]{0:T(128)S(1)} %pad_add_fusion.idx_ref, bf16[128,24576]{1,0:T(8,128)(2,1)} %hidden_hbm.1), custom_call_target="tpu_custom_call" | custom-call | flops 1 | bytes 1 | tf_op jit(solution)/shard_map/pack_hidden/pallas_call | solution.py:171
  8.5 2.9 %collective-permute-start = (bf16[128,2304]{1,0:T(8,128)(2,1)}, bf16[128,2304]{1,0:T(8,128)(2,1)S(1)}, u32[]{:S(2)}, u32[]{:S(2)}) collective-permute-start(bf16[128,2304]{1,0:T(8,128)(2,1)} %get-tuple-element.30), channel_id=1, source_target_pairs={{0,24},{8,16},{16,8},{24,0},{1,25},{9,17},{17,9},{25,1},{2,26},{10... | collective-permute-start | bytes 1769480 | tf_op jit(solution)/shard_map/ppermute | solution.py:342
  11.4 0.5 collective-permute-start.6
  11.9 0.0 collective-permute-done.2.refs_2_
  12.0 0.0 collective-permute-done.1.refs_1_
  12.0 3.5 %collective-permute-done.3.refs_3_ = bf16[128,768]{1,0:T(8,128)(2,1)S(1)} collective-permute-done((bf16[128,768]{1,0:T(8,128)(2,1)}, bf16[128,768]{1,0:T(8,128)(2,1)S(1)}, u32[]{:S(2)}, u32[]{:S(2)}) %collective-permute-start.3) | collective-permute-done | bytes 196640 | tf_op jit(solution)/shard_map/ppermute | solution.py:342
  15.5 14.2 %compress_codes.1 = (bf16[1,512,6144]{2,1,0:T(8,128)(2,1)}, bf16[128,1536]{1,0:T(8,128)(2,1)S(1)}, bf16[128,1536]{1,0:T(8,128)(2,1)S(1)}, bf16[128,1536]{1,0:T(8...) custom-call(s32[3]{0:T(128)S(1)} %pad_add_fusion.idx_ref, bf16[128,768]{1,0:T(8,128)(2,1)} %refs_0_.1, ...), custom_call_target="tpu_custom_call" | custom-call | flops 68719476736 | bytes 268435456 | tf_op jit(solution)/shard_map/compress_codes/pallas_call | solution.py:111
  29.7 0.1 collective-permute-start.4
  29.8 0.5 collective-permute-start.8
  30.3 0.0 collective-permute-done.diag
  30.3 1.2 %collective-permute-done.4 = bf16[128,1536]{1,0:T(8,128)(2,1)S(1)} collective-permute-done((bf16[128,1536]{1,0:T(8,128)(2,1)S(1)}, bf16[128,1536]{1,0:T(8,128)(2,1)S(1)}, u32[]{:S(2)}, u32[]{:S(2)}) %collective-permute-start.4) | collective-permute-done | bytes 393248 | tf_op jit(solution)/shard_map/ppermute | solution.py:345
  31.5 0.1 add_convert_fusion
  31.6 2.1 %collective-permute-start.9 = (bf16[128,1536]{1,0:T(8,128)(2,1)S(1)}, bf16[128,1536]{1,0:T(8,128)(2,1)S(1)}, u32[]{:S(2)}, u32[]{:S(2)}) collective-permute-start(bf16[128,1536]{1,0:T(8,128)(2,1)S(1)} %add_convert_fusion), channel_id=1, source_target_pairs={{0,2},{1,3},{2,0},{3,1},{4,6},{5,7},{6,4},{7,5},{8,10},{9,11},{10,... | collective-permute-start | bytes 1179656 | tf_op jit(solution)/shard_map/ppermute | solution.py:345
  33.7 1.5 %collective-permute-start.10 = (bf16[128,1536]{1,0:T(8,128)(2,1)S(1)}, bf16[128,1536]{1,0:T(8,128)(2,1)S(1)}, u32[]{:S(2)}, u32[]{:S(2)}) collective-permute-start(bf16[128,1536]{1,0:T(8,128)(2,1)S(1)} %copy-done.1), channel_id=1, source_target_pairs={{0,8},{1,17},{2,10},{3,19},{4,12},{5,21},{6,14},{7,23},{8,0},{9,25... | collective-permute-start | bytes 1179656 | tf_op jit(solution)/shard_map/ppermute | solution.py:367
  35.2 0.0 collective-permute-start.5
  35.2 4.6 %collective-permute-done.6.refs_0_ = bf16[128,4608]{1,0:T(8,128)(2,1)S(1)} collective-permute-done((bf16[128,4608]{1,0:T(8,128)(2,1)}, bf16[128,4608]{1,0:T(8,128)(2,1)S(1)}, u32[]{:S(2)}, u32[]{:S(2)}) %collective-permute-start.6) | collective-permute-done | bytes 1179680 | tf_op jit(solution)/shard_map/ppermute | solution.py:367
  39.8 0.1 convert_add_fusion
  39.9 0.0 copy-start
  39.9 2.1 %collective-permute-start.11 = (bf16[128,768]{1,0:T(8,128)(2,1)S(1)}, bf16[128,768]{1,0:T(8,128)(2,1)S(1)}, u32[]{:S(2)}, u32[]{:S(2)}) collective-permute-start(bf16[128,768]{1,0:T(8,128)(2,1)S(1)} %copy-done.2), channel_id=1, source_target_pairs={{0,24},{8,16},{16,8},{24,0},{1,25},{9,17},{17,9},{25,1},{2,26},{10... | collective-permute-start | bytes 589832 | tf_op jit(solution)/shard_map/ppermute | solution.py:342
  42.0 1.1 %collective-permute-done.9 = bf16[128,1536]{1,0:T(8,128)(2,1)S(1)} collective-permute-done((bf16[128,1536]{1,0:T(8,128)(2,1)S(1)}, bf16[128,1536]{1,0:T(8,128)(2,1)S(1)}, u32[]{:S(2)}, u32[]{:S(2)}) %collective-permute-start.9) | collective-permute-done | bytes 393248 | tf_op jit(solution)/shard_map/ppermute | solution.py:345
  43.1 0.1 fusion
  43.2 2.8 %collective-permute-start.12 = (bf16[64,1536]{1,0:T(8,128)(2,1)S(1)}, bf16[64,1536]{1,0:T(8,128)(2,1)S(1)}, u32[]{:S(2)}, u32[]{:S(2)}) collective-permute-start(bf16[64,1536]{1,0:T(8,128)(2,1)S(1)} %get-tuple-element.57), channel_id=1, source_target_pairs={{0,4},{1,5},{2,6},{3,7},{4,0},{5,1},{6,2},{7,3},{8,12},{9,13},{10,... | collective-permute-start | bytes 589832 | tf_op jit(solution)/shard_map/ppermute | solution.py:345
  46.0 7.2 %weight_gradient.2 = (bf16[6144,768]{1,0:T(8,128)(2,1)}, bf16[128,1536]{1,0:T(8,128)(2,1)S(1)}, bf16[512,768]{1,0:T(8,128)(2,1)S(1)}) custom-call(s32[3]{0:T(128)S(1)} %pad_add_fusion.idx_ref, bf16[128,24576]{1,0:T(8,128)(2,1)} %hidden_hbm.1, bf16[128,2304]{1,0:T(8,128)(2,1)S(1)} %collective-permute-done.diag, ...), custom_call_target="tpu_custom_call" | custom-call | flops 1 | bytes 1 | tf_op jit(solution)/shard_map/weight_gradient/pallas_call | solution.py:243
  53.2 0.1 collective-permute-start.13
  53.3 0.5 collective-permute-start.14
  53.8 1.0 %collective-permute-done.12.refs_1_ = bf16[64,1536]{1,0:T(8,128)(2,1)S(1)} collective-permute-done((bf16[64,1536]{1,0:T(8,128)(2,1)S(1)}, bf16[64,1536]{1,0:T(8,128)(2,1)S(1)}, u32[]{:S(2)}, u32[]{:S(2)}) %collective-permute-start.12) | collective-permute-done | bytes 196640 | tf_op jit(solution)/shard_map/ppermute | solution.py:345
  54.8 1.5 %grad_input.1 = bf16[64,6144]{1,0:T(8,128)(2,1)} custom-call(f32[64,1536]{1,0:T(8,128)S(1)} %get-tuple-element.46.refs_0_, bf16[64,1536]{1,0:T(8,128)(2,1)S(1)} %collective-permute-done.12.refs_1_, bf16[512,128]{1,0:T(8,128)(2,1)S(1)} %copy-done), custom_call_target="tpu_custom_call" | custom-call | flops 68719476736 | bytes 268435456 | tf_op jit(solution)/shard_map/grad_input/pallas_call | solution.py:322
  56.3 3.0 %weight_gradient.3 = bf16[6144,768]{1,0:T(8,128)(2,1)} custom-call(s32[3]{0:T(128)S(1)} %pad_add_fusion.idx_ref, bf16[128,1536]{1,0:T(8,128)(2,1)S(1)} %get-tuple-element.50.own, bf16[128,768]{1,0:T(8,128)(2,1)S(1)} %collective-permute-done.11.diag, bf16[128,768]{1,0:T(8,128)(2,1)S(1)} %collective-permute-done.13.swapped, ...), custom_call_target="tpu_custom_call", output_to_operand_aliasing={{}: (7, {})} | custom-call | flops 1 | bytes 1 | tf_op jit(solution)/shard_map/weight_gradient/pallas_call | solution.py:243
  (13 shorter events, 0.0 us)
Async XLA Ops:
  0.6 11.3 %collective-permute-start.2 = (bf16[128,768]{1,0:T(8,128)(2,1)}, bf16[128,768]{1,0:T(8,128)(2,1)S(1)}, u32[]{:S(2)}, u32[]{:S(2)}) collective-permute-start(bf16[128,768]{1,0:T(8,128)(2,1)} %refs_0_.1), channel_id=1, source_target_pairs={{0,16},{8,24},{16,0},{24,8},{1,17},{9,25},{17,1},{25,9},{2,18},{10... | collective-permute-start | bytes 589832 | tf_op jit(solution)/shard_map/ppermute | solution.py:342
  3.7 8.3 %collective-permute-start.1 = (bf16[128,768]{1,0:T(8,128)(2,1)}, bf16[128,768]{1,0:T(8,128)(2,1)S(1)}, u32[]{:S(2)}, u32[]{:S(2)}) collective-permute-start(bf16[128,768]{1,0:T(8,128)(2,1)} %refs_0_.1), channel_id=1, source_target_pairs={{0,8},{8,0},{16,24},{24,16},{1,9},{9,1},{17,25},{25,17},{2,10},{10... | collective-permute-start | bytes 589832 | tf_op jit(solution)/shard_map/ppermute | solution.py:342
  5.2 10.3 %collective-permute-start.3 = (bf16[128,768]{1,0:T(8,128)(2,1)}, bf16[128,768]{1,0:T(8,128)(2,1)S(1)}, u32[]{:S(2)}, u32[]{:S(2)}) collective-permute-start(bf16[128,768]{1,0:T(8,128)(2,1)} %refs_0_.1), channel_id=1, source_target_pairs={{0,24},{8,16},{16,8},{24,0},{1,25},{9,17},{17,9},{25,1},{2,26},{10... | collective-permute-start | bytes 589832 | tf_op jit(solution)/shard_map/ppermute | solution.py:342
  8.5 21.8 %collective-permute-start = (bf16[128,2304]{1,0:T(8,128)(2,1)}, bf16[128,2304]{1,0:T(8,128)(2,1)S(1)}, u32[]{:S(2)}, u32[]{:S(2)}) collective-permute-start(bf16[128,2304]{1,0:T(8,128)(2,1)} %get-tuple-element.30), channel_id=1, source_target_pairs={{0,24},{8,16},{16,8},{24,0},{1,25},{9,17},{17,9},{25,1},{2,26},{10... | collective-permute-start | bytes 1769480 | tf_op jit(solution)/shard_map/ppermute | solution.py:342
  11.4 22.3 %copy-start.1 = (bf16[128,1536]{1,0:T(8,128)(2,1)S(1)}, bf16[128,1536]{1,0:T(8,128)(2,1)}, u32[]{:S(2)}) copy-start(bf16[128,1536]{1,0:T(8,128)(2,1)} %get-tuple-element.44) | copy-start | bytes 1179652
  11.4 28.5 %copy-start.2 = (bf16[128,768]{1,0:T(8,128)(2,1)S(1)}, bf16[128,768]{1,0:T(8,128)(2,1)}, u32[]{:S(2)}) copy-start(bf16[128,768]{1,0:T(8,128)(2,1)} %get-tuple-element.45) | copy-start | bytes 589828
  11.4 28.4 %collective-permute-start.6 = (bf16[128,4608]{1,0:T(8,128)(2,1)}, bf16[128,4608]{1,0:T(8,128)(2,1)S(1)}, u32[]{:S(2)}, u32[]{:S(2)}) collective-permute-start(bf16[128,4608]{1,0:T(8,128)(2,1)} %get-tuple-element.34), channel_id=1, source_target_pairs={{0,8},{1,17},{2,10},{3,19},{4,12},{5,21},{6,14},{7,23},{8,0},{9,25... | collective-permute-start | bytes 3538952 | tf_op jit(solution)/shard_map/ppermute | solution.py:367
  29.7 1.8 %collective-permute-start.4 = (bf16[128,1536]{1,0:T(8,128)(2,1)S(1)}, bf16[128,1536]{1,0:T(8,128)(2,1)S(1)}, u32[]{:S(2)}, u32[]{:S(2)}) collective-permute-start(bf16[128,1536]{1,0:T(8,128)(2,1)S(1)} %get-tuple-element.31), channel_id=1, source_target_pairs={{0,1},{1,0},{2,3},{3,2},{4,5},{5,4},{6,7},{7,6},{8,9},{9,8},{10,11... | collective-permute-start | bytes 1179656 | tf_op jit(solution)/shard_map/ppermute | solution.py:345
  29.8 10.0 %collective-permute-start.8 = (bf16[128,1536]{1,0:T(8,128)(2,1)S(1)}, bf16[128,1536]{1,0:T(8,128)(2,1)S(1)}, u32[]{:S(2)}, u32[]{:S(2)}) collective-permute-start(bf16[128,1536]{1,0:T(8,128)(2,1)S(1)} %get-tuple-element.39), channel_id=1, source_target_pairs={{0,1},{1,0},{2,3},{3,2},{4,5},{5,4},{6,7},{7,6},{8,9},{9,8},{10,11... | collective-permute-start | bytes 1179656 | tf_op jit(solution)/shard_map/ppermute | solution.py:345
  31.6 11.5 %collective-permute-start.9 = (bf16[128,1536]{1,0:T(8,128)(2,1)S(1)}, bf16[128,1536]{1,0:T(8,128)(2,1)S(1)}, u32[]{:S(2)}, u32[]{:S(2)}) collective-permute-start(bf16[128,1536]{1,0:T(8,128)(2,1)S(1)} %add_convert_fusion), channel_id=1, source_target_pairs={{0,2},{1,3},{2,0},{3,1},{4,6},{5,7},{6,4},{7,5},{8,10},{9,11},{10,... | collective-permute-start | bytes 1179656 | tf_op jit(solution)/shard_map/ppermute | solution.py:345
  33.7 19.5 %collective-permute-start.10 = (bf16[128,1536]{1,0:T(8,128)(2,1)S(1)}, bf16[128,1536]{1,0:T(8,128)(2,1)S(1)}, u32[]{:S(2)}, u32[]{:S(2)}) collective-permute-start(bf16[128,1536]{1,0:T(8,128)(2,1)S(1)} %copy-done.1), channel_id=1, source_target_pairs={{0,8},{1,17},{2,10},{3,19},{4,12},{5,21},{6,14},{7,23},{8,0},{9,25... | collective-permute-start | bytes 1179656 | tf_op jit(solution)/shard_map/ppermute | solution.py:367
  35.2 10.8 %collective-permute-start.5 = (bf16[128,2304]{1,0:T(8,128)(2,1)S(1)}, bf16[128,2304]{1,0:T(8,128)(2,1)S(1)}, u32[]{:S(2)}, u32[]{:S(2)}) collective-permute-start(bf16[128,2304]{1,0:T(8,128)(2,1)S(1)} %collective-permute-done.diag), channel_id=1, source_target_pairs={{0,1},{1,0},{2,3},{3,2},{4,5},{5,4},{6,7},{7,6},{8,9},{9,8},{10,11... | collective-permute-start | bytes 1769480 | tf_op jit(solution)/shard_map/ppermute | solution.py:345
  39.8 6.2 %collective-permute-start.7 = (bf16[128,4608]{1,0:T(8,128)(2,1)S(1)}, bf16[128,4608]{1,0:T(8,128)(2,1)S(1)}, u32[]{:S(2)}, u32[]{:S(2)}) collective-permute-start(bf16[128,4608]{1,0:T(8,128)(2,1)S(1)} %collective-permute-done.6.refs_0_), channel_id=1, source_target_pairs={{0,1},{1,0},{2,3},{3,2},{4,5},{5,4},{6,7},{7,6},{8,9},{9,8},{10,11... | collective-permute-start | bytes 3538952 | tf_op jit(solution)/shard_map/ppermute | solution.py:345
  39.9 14.9 %copy-start = (bf16[512,128]{1,0:T(8,128)(2,1)S(1)}, bf16[512,128]{1,0:T(8,128)(2,1)}, u32[]{:S(2)}) copy-start(bf16[512,128]{1,0:T(8,128)(2,1)} %refs_2_.1) | copy-start | bytes 393220
  39.9 13.3 %collective-permute-start.11 = (bf16[128,768]{1,0:T(8,128)(2,1)S(1)}, bf16[128,768]{1,0:T(8,128)(2,1)S(1)}, u32[]{:S(2)}, u32[]{:S(2)}) collective-permute-start(bf16[128,768]{1,0:T(8,128)(2,1)S(1)} %copy-done.2), channel_id=1, source_target_pairs={{0,24},{8,16},{16,8},{24,0},{1,25},{9,17},{17,9},{25,1},{2,26},{10... | collective-permute-start | bytes 589832 | tf_op jit(solution)/shard_map/ppermute | solution.py:342
  43.2 11.6 %collective-permute-start.12 = (bf16[64,1536]{1,0:T(8,128)(2,1)S(1)}, bf16[64,1536]{1,0:T(8,128)(2,1)S(1)}, u32[]{:S(2)}, u32[]{:S(2)}) collective-permute-start(bf16[64,1536]{1,0:T(8,128)(2,1)S(1)} %get-tuple-element.57), channel_id=1, source_target_pairs={{0,4},{1,5},{2,6},{3,7},{4,0},{5,1},{6,2},{7,3},{8,12},{9,13},{10,... | collective-permute-start | bytes 589832 | tf_op jit(solution)/shard_map/ppermute | solution.py:345
  53.2 3.1 %collective-permute-start.13 = (bf16[128,768]{1,0:T(8,128)(2,1)S(1)}, bf16[128,768]{1,0:T(8,128)(2,1)S(1)}, u32[]{:S(2)}, u32[]{:S(2)}) collective-permute-start(bf16[128,768]{1,0:T(8,128)(2,1)S(1)} %collective-permute-done.11.diag), channel_id=1, source_target_pairs={{0,1},{1,0},{2,3},{3,2},{4,5},{5,4},{6,7},{7,6},{8,9},{9,8},{10,11... | collective-permute-start | bytes 589832 | tf_op jit(solution)/shard_map/ppermute | solution.py:345
  53.3 3.0 %collective-permute-start.14 = (bf16[128,1536]{1,0:T(8,128)(2,1)S(1)}, bf16[128,1536]{1,0:T(8,128)(2,1)S(1)}, u32[]{:S(2)}, u32[]{:S(2)}) collective-permute-start(bf16[128,1536]{1,0:T(8,128)(2,1)S(1)} %collective-permute-done.10.refs_0_), channel_id=1, source_target_pairs={{0,1},{1,0},{2,3},{3,2},{4,5},{5,4},{6,7},{7,6},{8,9},{9,8},{10,11... | collective-permute-start | bytes 1179656 | tf_op jit(solution)/shard_map/ppermute | solution.py:345
